TPU v7x, 256 devices: a whole 4x4x8 slice. The times are simulated.
256 devices in a mesh: dp: 32 (over y, z), tensor: 8 (over x, core).
Axes of the slice: x: 4, y: 4, z: 8, core: 2. Of those that a mesh axis runs over, the one named last changes fastest.
Arguments:
- saved_master: float32 [8, 128, 73728], P('tensor', 'dp'), may hold values from -0.078125 to 0.078125
- saved_first: float32 [8, 128, 73728], P('tensor', 'dp'), may hold values from -6 to 6
- saved_second: float32 [8, 128, 73728], P('tensor', 'dp'), may hold values from 0.25 to 4
- piece_columns: int32 [8, 128], P('tensor'), may hold values from 1 to 96, 6144 in all within a row
- load_order: int32 [8, 128], P('tensor'), may hold values from 0 to 127, each once within a row
- context: bfloat16 [8192, 6144], P('dp', 'tensor'), may hold values from -6 to 6
- out_grad: bfloat16 [8192, 6144], P('dp'), may hold values from -0.26367188 to 0.26367188
- next_context: bfloat16 [16384, 6144], P('dp', 'tensor'), may hold values from -6 to 6
Outputs:
- new_master: float32 [6144, 6144], P(('tensor', 'dp'))
- new_first: float32 [6144, 6144], P(('tensor', 'dp'))
- new_second: float32 [6144, 6144], P(('tensor', 'dp'))
- activations: bfloat16 [16384, 6144], P('dp', 'tensor')
Inputs may be any that keep to these rules, and one draw needn't show every extreme that they name: `piece_columns`: for each tensor index the pieces lie one after another in old-rank order and cover all 6144 columns; some piece holds exactly 96 columns. `load_order`: for each tensor index every old rank sits at exactly one saved position.
All inputs are finite; a program needn't handle non-finite values.
Results may differ from a plain program's by a relative error of at most 0.0049.
Values may be sent and summed in bfloat16 or wider, within the bound.
A program may use at most 128 MiB of HBM per device.

v0:
```python
import jax
import jax.numpy as jnp
from jax import lax
from jax.sharding import PartitionSpec as P

first_bias = 1.0 - 0.9**20
second_bias = 1.0 - 0.95**20


def locate(lengths, order, total_columns, widest):
    old_ranks = lengths.shape[0]
    starts = jnp.cumsum(lengths) - lengths
    columns = jnp.arange(total_columns, dtype=jnp.int32)
    owner_rank = jnp.sum((starts[None, :] <= columns[:, None]).astype(jnp.int32), axis=1) - 1
    places = jnp.arange(old_ranks, dtype=jnp.int32)
    position = jnp.sum(jnp.where(order[None, :] == places[:, None], places[None, :], 0), axis=1)
    picked = owner_rank[:, None] == places[None, :]
    slot_of = jnp.sum(jnp.where(picked, position[None, :], 0), axis=1)
    start_of = jnp.sum(jnp.where(picked, starts[None, :], 0), axis=1)
    return slot_of * widest + columns - start_of


def shards(
    saved_master,
    saved_first,
    saved_second,
    piece_columns,
    load_order,
    context,
    out_grad,
    next_context,
):
    dp_size = lax.axis_size("dp")
    slot_count = saved_master.shape[1]
    rows_local = context.shape[1]
    total_columns = out_grad.shape[1]
    widest = saved_master.shape[2] // rows_local
    row_band = rows_local // dp_size
    send_master = saved_master.reshape(slot_count, dp_size, row_band * widest)
    send_first = saved_first.reshape(slot_count, dp_size, row_band * widest)
    send_second = saved_second.reshape(slot_count, dp_size, row_band * widest)
    got_master, got_first, got_second = (
        lax.all_to_all(send_master, "dp", split_axis=1, concat_axis=0, tiled=True),
        lax.all_to_all(send_first, "dp", split_axis=1, concat_axis=0, tiled=True),
        lax.all_to_all(send_second, "dp", split_axis=1, concat_axis=0, tiled=True),
    )
    source = locate(piece_columns[0], load_order[0], total_columns, widest)

    def assemble(received):
        old_ranks = received.shape[0]
        flat_rows = (
            received.reshape(old_ranks, row_band, widest)
            .transpose(1, 0, 2)
            .reshape(row_band, old_ranks * widest)
        )
        return jnp.take(flat_rows, source, axis=1)

    master = assemble(got_master)
    first_moment = assemble(got_first)
    second_moment = assemble(got_second)
    gradient = lax.psum_scatter(
        lax.dot_general(
            context, out_grad, (((0,), (0,)), ((), ())), preferred_element_type=jnp.float32
        ),
        "dp",
        scatter_dimension=0,
        tiled=True,
    )
    new_first = 0.9 * first_moment + 0.1 * gradient
    new_second = 0.95 * second_moment + 0.05 * gradient * gradient
    new_master = master - 0.01 * (new_first / first_bias) / (
        jnp.sqrt(new_second / second_bias) + 1e-08
    )
    weight = new_master.astype(jnp.bfloat16)
    full_rows = lax.all_gather(weight, "dp", axis=0, tiled=True)
    partial_out = jnp.dot(next_context, full_rows, preferred_element_type=jnp.float32)
    summed = lax.psum_scatter(partial_out, "tensor", scatter_dimension=1, tiled=True)
    activations = summed.astype(jnp.bfloat16)
    return (new_master, new_first, new_second, activations)


def solution(mesh):
    placed = (
        P("tensor", "dp", None),
        P("tensor", "dp", None),
        P("tensor", "dp", None),
        P("tensor", None),
        P("tensor", None),
        P("dp", "tensor"),
        P("dp", None),
        P("dp", "tensor"),
    )
    return jax.shard_map(
        shards,
        mesh=mesh,
        in_specs=placed,
        out_specs=(
            P(("tensor", "dp"), None),
            P(("tensor", "dp"), None),
            P(("tensor", "dp"), None),
            P("dp", "tensor"),
        ),
        check_vma=False,
    )
```

profile of v0, /device:TPU:8, one launch (start us, length us, event | category | flops | bytes accessed | tf_op | source)
XLA Modules:
  0.0 530.3 jit_solution(4311254743694406258)
XLA Ops:
  7.2 0.0 copy-start
  7.2 0.0 reduce-scatter.3.cloned.1.call-start
  7.2 1.8 copy-done
  9.1 8.8 %fusion.5 = f32[768,6144]{1,0:T(8,128)} fusion(bf16[256,768]{1,0:T(8,128)(2,1)} %param.15, bf16[256,6144]{1,0:T(8,128)(2,1)S(1)} %copy-done), kind=kOutput, calls=%fused_computation.23 | convolution fusion | flops 2415919104 | bytes 22413312 | tf_op jit(solution)/shard_map/dot_general | solution.py:62
  17.9 0.0 copy-start.2
  17.9 0.0 reduce-scatter.3.cloned.1.call-update
  17.9 0.0 copy-start.3
  17.9 1.2 copy-done.2
  19.2 0.0 copy-start.6
  19.2 0.0 copy-start.5
  19.2 54.9 %all_to_all.45 = f32[4,32,2304]{2,0,1:T(4,128)} all-to-all(f32[4,32,2304]{2,0,1:T(4,128)S(1)} %bitcast.54), channel_id=1, replica_groups=mesh['dp'=32,'tensor'=8] {'dp'}, dimensions={1} | all-to-all | bytes 2359296 | tf_op jit(solution)/shard_map/all_to_all | solution.py:44
  74.1 0.0 copy-done.3
  74.1 48.9 %all_to_all.46 = f32[4,32,2304]{2,0,1:T(4,128)S(1)} all-to-all(f32[4,32,2304]{2,0,1:T(4,128)S(1)} %bitcast.55), channel_id=1, replica_groups=mesh['dp'=32,'tensor'=8] {'dp'}, dimensions={1} | all-to-all | bytes 2359296 | tf_op jit(solution)/shard_map/all_to_all | solution.py:45
  123.0 6.1 %all-to-all-start = ((f32[4,32,2304]{2,0,1:T(4,128)}), f32[4,32,2304]{2,0,1:T(4,128)}, u32[]{:S(2)}, u32[]{:S(2)}) async-start(f32[4,32,2304]{2,0,1:T(4,128)} %bitcast.56), calls=%async_computation | async-start | bytes 2359296 | tf_op jit(solution)/shard_map/all_to_all | solution.py:43
  129.1 0.2 all-gather.2.cloned.1.call-start
  129.3 0.0 copy-done.6
  129.3 0.3 reduce-window_clone.1
  129.6 0.0 copy-done.5
  129.6 0.1 select_reduce_fusion.2
  129.7 0.9 convert_reduce_fusion
  130.7 4.6 select_reduce_fusion.1
  135.3 1.3 reshape.60
  136.7 2.6 reshape.57
  139.2 30.3 %all-to-all-done = f32[4,32,2304]{2,0,1:T(4,128)} async-done(((f32[4,32,2304]{2,0,1:T(4,128)}), f32[4,32,2304]{2,0,1:T(4,128)}, u32[]{:S(2)}, u32[]{:S(2)}) %all-to-all-start) | async-done | bytes 1179680 | tf_op jit(solution)/shard_map/all_to_all | solution.py:43
  169.6 3.4 reshape.54
  173.0 5.1 copy.27
  178.1 23.8 %gather_fusion = f32[6144,24]{1,0:T(8,128)} fusion(f32[24,12288]{0,1:T(8,128)} %bitcast.47, s32[6144]{0:T(1024)S(1)} %broadcast_clamp_fusion), kind=kCustom, calls=%fused_computation.clone | custom fusion | bytes 1204224 | tf_op jit(solution)/shard_map/jit(_take)/gather | solution.py:56
  201.8 3.1 copy.28
  204.9 4.0 copy.30
  208.9 23.8 %gather_fusion.1 = f32[6144,24]{1,0:T(8,128)} fusion(f32[24,12288]{0,1:T(8,128)} %bitcast.48, s32[6144]{0:T(1024)S(1)} %broadcast_clamp_fusion), kind=kCustom, calls=%fused_computation.1.clone | custom fusion | bytes 1204224 | tf_op jit(solution)/shard_map/jit(_take)/gather | solution.py:56
  232.7 3.0 copy.31
  235.8 4.0 copy.33
  239.8 18.9 %gather_fusion.2 = f32[6144,24]{1,0:T(8,128)S(1)} fusion(f32[24,12288]{0,1:T(8,128)} %bitcast.46, s32[6144]{0:T(1024)S(1)} %broadcast_clamp_fusion), kind=kCustom, calls=%fused_computation.2.clone | custom fusion | bytes 1204224 | tf_op jit(solution)/shard_map/jit(_take)/gather | solution.py:56
  258.7 1.8 copy.34
  260.5 0.0 copy-start.4
  260.5 68.5 %reduce-scatter.3.cloned.1.call-done = f32[24,6144]{1,0:T(8,128)} async-done(((f32[768,6144]{1,0:T(8,128)}), f32[24,6144]{1,0:T(8,128)}) %reduce-scatter.3.cloned.1.call-update) | async-done | bytes 589840 | tf_op jit(solution)/shard_map/reduce_scatter | solution.py:61
  329.0 3.2 fusion.2
  332.2 0.0 all-gather.2.cloned.1.call-update
  332.2 0.3 reduce-scatter.5.cloned.1.call-start
  332.5 101.4 %all-gather.2.cloned.1.call-done = bf16[768,6144]{1,0:T(8,128)(2,1)} async-done(((bf16[24,6144]{1,0:T(8,128)(2,1)}), bf16[768,6144]{1,0:T(8,128)(2,1)}) %all-gather.2.cloned.1.call-update) | async-done | bytes 9437200 | tf_op jit(solution)/shard_map/all_gather | solution.py:75
  433.8 0.0 copy-done.4
  433.8 11.9 %convolution_bitcast_fusion = f32[512,6144]{0,1:T(8,128)} fusion(bf16[768,6144]{1,0:T(8,128)(2,1)} %all-gather.2.cloned.1.call-done, bf16[512,768]{1,0:T(8,128)(2,1)S(1)} %copy-done.4), kind=kOutput, calls=%fused_computation.3 | convolution fusion | flops 4831838208 | bytes 22806528 | tf_op jit(solution)/shard_map/dot_general | solution.py:76
  445.7 0.0 reduce-scatter.5.cloned.1.call-update
  445.7 0.0 copy-start.1
  445.8 73.4 %reduce-scatter.5.cloned.1.call-done = f32[512,768]{0,1:T(8,128)} async-done(((f32[512,6144]{0,1:T(8,128)}), f32[512,768]{0,1:T(8,128)}) %reduce-scatter.5.cloned.1.call-update) | async-done | bytes 1572880 | tf_op jit(solution)/shard_map/reduce_scatter | solution.py:77
  519.1 2.4 convert_element_type.11
  521.5 2.3 copy.35
  523.8 0.0 copy-done.1
  (4 shorter events, 0.0 us)
Async XLA Ops:
  7.2 1.9 copy-start
  7.2 321.8 %reduce-scatter.3.cloned.1.call-start = ((), (), s32[]{:S(2)}) async-start(), calls=%async_computation.5 | async-start | bytes 19464192 | tf_op jit(solution)/shard_map/reduce_scatter | solution.py:61
  17.9 1.3 copy-start.2
  17.9 56.2 %copy-start.3 = (f32[1,4,73728]{2,1,0:T(4,128)S(1)}, f32[1,4,73728]{2,1,0:T(4,128)}, u32[]{:S(2)}) copy-start(f32[1,4,73728]{2,1,0:T(4,128)} %param.12) | copy-start | bytes 3538948
  19.2 110.2 %copy-start.6 = (s32[1,128]{1,0:T(1,128)S(1)}, s32[1,128]{1,0:T(1,128)}, u32[]{:S(2)}) copy-start(s32[1,128]{1,0:T(1,128)} %param.13) | copy-start | bytes 1540
  19.2 110.5 %copy-start.5 = (s32[1,128]{1,0:T(1,128)S(1)}, s32[1,128]{1,0:T(1,128)}, u32[]{:S(2)}) copy-start(s32[1,128]{1,0:T(1,128)} %param.14) | copy-start | bytes 1540
  123.0 46.6 %all-to-all-start = ((f32[4,32,2304]{2,0,1:T(4,128)}), f32[4,32,2304]{2,0,1:T(4,128)}, u32[]{:S(2)}, u32[]{:S(2)}) async-start(f32[4,32,2304]{2,0,1:T(4,128)} %bitcast.56), calls=%async_computation | async-start | bytes 2359296 | tf_op jit(solution)/shard_map/all_to_all | solution.py:43
  129.1 304.8 %all-gather.2.cloned.1.call-start = ((), (), s32[]{:S(2)}) async-start(), calls=%async_computation.6 | async-start | bytes 9732096 | tf_op jit(solution)/shard_map/all_gather | solution.py:75
  260.5 173.3 %copy-start.4 = (bf16[512,768]{1,0:T(8,128)(2,1)S(1)}, bf16[512,768]{1,0:T(8,128)(2,1)}, u32[]{:S(2)}) copy-start(bf16[512,768]{1,0:T(8,128)(2,1)} %param.17) | copy-start | bytes 2359300
  332.2 186.9 %reduce-scatter.5.cloned.1.call-start = ((), (), s32[]{:S(2)}) async-start(), calls=%async_computation.7 | async-start | bytes 14155776 | tf_op jit(solution)/shard_map/reduce_scatter | solution.py:77
  445.7 78.1 %copy-start.1 = (bf16[256,6144]{1,0:T(8,128)(2,1)S(1)}, bf16[256,6144]{1,0:T(8,128)(2,1)}, u32[]{:S(2)}) copy-start(bf16[256,6144]{1,0:T(8,128)(2,1)} %param.16) | copy-start | bytes 9437188
Sparse Core Ops, SparseCore 0:
  18.0 310.9 reduce-scatter.2
  332.3 101.4 all-gather.1
  445.9 73.2 reduce-scatter.4
where the time goes:
time: 531 us; the launch traced here: 530 us
  waiting for transfers between devices  274 us (52%)
  blocking collectives  104 us (20%)
  local copies, waits for them, and re-layouts  100 us (19%)
  matrix products  20.7 us (4%)
  between operations  13.9 us (3%)
  other arithmetic  11.6 us (2%)
  starting transfers between devices  6.59 us (1%)
    all_gather x1, waiting for transfers between devices, shards(): full_rows = lax.all_gather(weight, 'dp', axis=0, tiled=True)  101 us
    gather x6, local copies, waits for them, and re-layouts, assemble(): return jnp.take(flat_rows, source, axis=1)  74.4 us
    reduce_scatter x1, waiting for transfers between devices, shards(): lax.psum_scatter(partial_out, 'tensor', scatter_dimension=1, tiled=True)  73.4 us
    reduce_scatter x1, waiting for transfers between devices, shards(): lax.psum_scatter(lax.dot_general(context, out_grad, (((0,), (0,)), ((), (...  68.5 us
    all_to_all x1, blocking collectives, shards(): lax.all_to_all(send_first, 'dp', split_axis=1, concat_axis=0, tiled=True)  54.9 us
    all_to_all x1, blocking collectives, shards(): lax.all_to_all(send_second, 'dp', split_axis=1, concat_axis=0, tiled=True)  48.9 us
    all_to_all x1, waiting for transfers between devices, shards(): lax.all_to_all(send_master, 'dp', split_axis=1, concat_axis=0, tiled=True)  30.3 us
    transpose x3, local copies, waits for them, and re-layouts, assemble(): flat_rows = received.reshape(old_ranks, row_band, widest).transpose(1, 0,...  13.1 us
  transfers between devices with their start and end apart: 4, of which 4 were waited for; matrix products, arithmetic and copies ran while one was open for 19% of the time, Pallas kernels for 0%

commit v1 on v0

v1 whole, which is shorter than its diff:
```python
import jax
import jax.numpy as jnp
from jax import lax
from jax.experimental import pallas as pl
from jax.experimental.pallas import tpu as pltpu
from jax.sharding import PartitionSpec as P

first_bias = 1.0 - 0.9**20
second_bias = 1.0 - 0.95**20

MESH = pl.DeviceIdType.MESH
BF = jnp.bfloat16
F32 = jnp.float32
NY, NZ = 4, 8
NT = 8
BAND = 24
WIDE = 384
GROUPS = 6
SROWS = 80
QUARTER = 1536
HALF = 768


def where_am_i():
    dp = lax.axis_index("dp")
    t = lax.axis_index("tensor")
    return dp, t, dp // NZ, lax.rem(dp, NZ)


def remote(src, dst, send, recv, device):
    return pltpu.make_async_remote_copy(
        src_ref=src, dst_ref=dst, send_sem=send, recv_sem=recv, device_id=device, device_id_type=MESH
    )


def kernel_a(
    sm, sf, ss, ctx, og, rx, gq,
    st, flat, tx, cg, ct, oq, grad, zs, zr, tot, ysb,
    load_sem, loc_sem, st_s, st_r, cx_s, cx_r, og_s, og_r, fw_s, fw_r, rs_s, rs_r, ya_s, ya_r,
):
    dp, t, y, z = where_am_i()
    core = lax.rem(t, 2)
    mate = t + 1 - 2 * core

    loads = [pltpu.make_async_copy(src, st.at[a], load_sem.at[a]) for a, src in enumerate((sm, sf, ss))]
    for copy in loads:
        copy.start()
    own_ctx = pltpu.make_async_copy(ctx, cg.at[pl.ds(y * 256, 256)], loc_sem.at[0])
    own_og = pltpu.make_async_copy(
        og.at[:, pl.ds(y * QUARTER, QUARTER)], oq.at[pl.ds(y * 256, 256)], loc_sem.at[1]
    )
    own_ctx.start()
    own_og.start()

    barrier = pltpu.get_barrier_semaphore()

    @pl.loop(1, 32)
    def _(i):
        pl.semaphore_signal(barrier, inc=1, device_id=(lax.rem(dp + i, 32), t), device_id_type=MESH)

    pl.semaphore_signal(barrier, inc=1, device_id=(dp, mate), device_id_type=MESH)
    pl.semaphore_wait(barrier, 32)

    def ctx_copy(k):
        to = lax.rem(y + k, NY)
        return remote(ctx, cg.at[pl.ds(y * 256, 256)], cx_s.at[k], cx_r.at[k], (to * NZ + z, t))

    def og_copy(k):
        to = lax.rem(y + k, NY)
        return remote(
            og.at[pl.ds(core * 128, 128), pl.ds(to * QUARTER, QUARTER)],
            oq.at[pl.ds(y * 256 + core * 128, 128)],
            og_s.at[k], og_r.at[k], (to * NZ + z, t),
        )

    def fw_copy(k):
        rows = pl.ds(lax.rem(y + NY - k, NY) * 256 + core * 128, 128)
        return remote(oq.at[rows], oq.at[rows], fw_s.at[k], fw_r.at[k], (dp, mate))

    for k in (2, 1, 3):
        og_copy(k).start()
        ctx_copy(k).start()

    for copy in loads:
        copy.wait()

    def state_copy(i):
        to = lax.rem(y + i // NZ, NY) * NZ + lax.rem(z + lax.rem(i, NZ), NZ)
        return to, remote(tx.at[to], rx.at[dp], st_s.at[i], st_r.at[i], (to, t))

    def build(to):
        for a in range(3):
            for g in range(GROUPS):
                flat[a * BAND + 4 * g : a * BAND + 4 * g + 4, :] = st[a, to * GROUPS + g]
        tx[to] = flat[...].astype(BF)

    flat[3 * BAND :, :] = jnp.zeros((SROWS - 3 * BAND, WIDE), F32)

    @pl.loop(1, 32)
    def _(i):
        to, copy = state_copy(i)
        build(to)
        copy.start()

    build(dp)
    own_state = pltpu.make_async_copy(tx.at[dp], rx.at[dp], loc_sem.at[2])
    own_state.start()

    own_ctx.wait()
    own_og.wait()

    def turn(source):
        ct[:, pl.ds(source * 256, 256)] = cg[pl.ds(source * 256, 256), :].T

    turn(y)
    for k in (1, 3, 2):
        og_copy(k).wait_recv()
        fw_copy(k).start()
    for k in (1, 3, 2):
        ctx_copy(k).wait_recv()
        turn(lax.rem(y + NY - k, NY))
    for k in (1, 3, 2):
        fw_copy(k).wait_recv()

    def chunk(dest, h):
        return jnp.concatenate(
            [grad[pl.ds((yy * NZ + dest) * BAND, BAND), h * HALF : (h + 1) * HALF] for yy in range(NY)], axis=0
        )

    def steps(d, h):
        return 4 if d == h else 3

    def ring_copy(d, h, s):
        to = lax.rem(z + (1 if d == 0 else NZ - 1), NZ)
        return remote(zs.at[d, h, s], zr.at[d, h, s], rs_s.at[d, h, s], rs_r.at[d, h, s], (y * NZ + to, t))

    def ring_send(d, h, s):
        sign = 1 if d == 0 else NZ - 1
        dest = lax.rem(z + sign * (steps(d, h) - s), NZ)
        value = chunk(dest, h)
        if s > 0:
            ring_copy(d, h, s - 1).wait_recv()
            value = value + zr[d, h, s - 1].astype(F32)
        zs[d, h, s] = value.astype(BF)
        ring_copy(d, h, s).start()

    for h in range(2):
        @pl.loop(0, 3)
        def _(n):
            cols = pl.ds(h * HALF + n * 256, 256)
            grad[:, cols] = jnp.dot(ct[...], oq[:, cols], preferred_element_type=F32)

        ring_send(h, h, 0)
        ring_send(1 - h, h, 0)

    for s in range(1, 4):
        for h in range(2):
            for d in (h, 1 - h):
                if s < steps(d, h):
                    ring_send(d, h, s)

    def out_copy(k, h):
        to = lax.rem(y + k, NY)
        return remote(ysb.at[k, h], gq.at[y, h], ya_s.at[k, h], ya_r.at[k, h], (to * NZ + z, t))

    own_out = []
    for h in range(2):
        value = chunk(z, h)
        for d in (1 - h, h):
            last = steps(d, h) - 1
            ring_copy(d, h, last).wait_recv()
            value = value + zr[d, h, last].astype(F32)
        tot[...] = value
        for k in (2, 1, 3, 0):
            rows = pl.ds(lax.rem(y + k, NY) * BAND, BAND)
            ysb[k, h] = jnp.concatenate([tot[rows, 0:WIDE], tot[rows, WIDE:HALF]], axis=0).astype(BF)
            if k:
                out_copy(k, h).start()
            else:
                own_out.append(pltpu.make_async_copy(ysb.at[0, h], gq.at[y, h], loc_sem.at[3 + h]))
                own_out[-1].start()

    for k in (1, 2, 3):
        og_copy(k).wait_send()
        ctx_copy(k).wait_send()
        fw_copy(k).wait_send()
    for h in range(2):
        for d in range(2):
            for s in range(steps(d, h)):
                ring_copy(d, h, s).wait_send()
        for k in (1, 2, 3):
            out_copy(k, h).wait()
        own_out[h].wait()
    own_state.wait()

    @pl.loop(1, 32)
    def _(i):
        _, copy = state_copy(i)
        copy.wait()


def run_a(sm, sf, ss, ctx, og):
    any_spec = pl.BlockSpec(memory_space=pl.ANY)
    dma = pltpu.SemaphoreType.DMA
    return pl.pallas_call(
        kernel_a,
        name="state_and_gradient",
        out_shape=(
            jax.ShapeDtypeStruct((32, SROWS, WIDE), BF),
            jax.ShapeDtypeStruct((NY, 2, 2 * BAND, WIDE), BF),
        ),
        in_specs=[any_spec] * 5,
        out_specs=(any_spec, any_spec),
        scratch_shapes=[
            pltpu.VMEM((3, 192, 4, WIDE), F32),
            pltpu.VMEM((SROWS, WIDE), F32),
            pltpu.VMEM((32, SROWS, WIDE), BF),
            pltpu.VMEM((1024, HALF), BF),
            pltpu.VMEM((HALF, 1024), BF),
            pltpu.VMEM((1024, QUARTER), BF),
            pltpu.VMEM((HALF, QUARTER), F32),
            pltpu.VMEM((2, 2, 4, 4 * BAND, HALF), BF),
            pltpu.VMEM((2, 2, 4, 4 * BAND, HALF), BF),
            pltpu.VMEM((4 * BAND, HALF), F32),
            pltpu.VMEM((4, 2, 2 * BAND, WIDE), BF),
            dma((3,)), dma((5,)),
            dma((32,)), dma((32,)),
            dma((4,)), dma((4,)), dma((4,)), dma((4,)), dma((4,)), dma((4,)),
            dma((2, 2, 4)), dma((2, 2, 4)),
            dma((4, 2)), dma((4, 2)),
        ],
        compiler_params=pltpu.CompilerParams(
            collective_id=0, has_side_effects=True, vmem_limit_bytes=48 * 2**20
        ),
        cost_estimate=pl.CostEstimate(flops=2 * 1024 * 768 * 1536, bytes_accessed=16 * 2**20, transcendentals=0),
    )(sm, sf, ss, ctx, og)


def kernel_b(pc, lo, rx, gq, nm, nf, ns, wb, zbuf, obuf, gbuf, mbuf, fbuf, sbuf, starts, sem):
    row = lax.broadcasted_iota(jnp.int32, (WIDE, 512), 0)
    col = lax.broadcasted_iota(jnp.int32, (WIDE, 512), 1)
    spread = ((row == (col // 128) * 96 + lax.rem(col, 128)) & (lax.rem(col, 128) < 96)).astype(BF)

    def count(j, total):
        starts[j] = total
        return total + pc[j]

    lax.fori_loop(0, 128, count, jnp.int32(0))

    @pl.loop(0, 10)
    def _(i):
        rows = pl.ds(i * 256, 256)
        value = jnp.dot(rx[rows, :], spread, preferred_element_type=F32)
        for r in range(4):
            zbuf[r, rows, :] = value[:, r * 128 : (r + 1) * 128]

    for yy in range(NY):
        for h in range(2):
            block = gq[yy, h].astype(F32)
            for q in range(2):
                c0 = yy * QUARTER + h * HALF + q * WIDE
                for n in range(3):
                    gbuf[c0 // 128 + n, 0:BAND, :] = block[q * BAND : (q + 1) * BAND, n * 128 : (n + 1) * 128]

    lane = lax.broadcasted_iota(jnp.int32, (8, 128), 1)

    @pl.loop(0, 128)
    def _(i):
        rank = lo[i]
        start = starts[rank]
        length = pc[rank]
        tile = start // 128
        offset = lax.rem(start, 128)
        keep = (lane >= offset) & (lane < offset + length)
        spill = lane < offset + length - 128
        base = (i // 4) * SROWS + lax.rem(i, 4)
        for a in range(3):
            for r in range(4):
                value = zbuf[r, pl.ds(base + a * BAND, 8, stride=4), :]
                value = pltpu.roll(value, offset, 1)
                pltpu.store(obuf.at[a * 4 + r, tile], value, mask=keep)
                pltpu.store(obuf.at[a * 4 + r, tile + 1], value, mask=spill)

    @pl.loop(0, 48)
    def _(n):
        cols = pl.ds(pl.multiple_of(n * 128, 128), 128)
        for r in range(4):
            rows = pl.ds(r, 8, stride=4)
            gradient = gbuf[n, rows, :]
            first = 0.9 * obuf[4 + r, n] + 0.1 * gradient
            second = 0.95 * obuf[8 + r, n] + 0.05 * gradient * gradient
            master = obuf[r, n] - 0.01 * (first / first_bias) / (jnp.sqrt(second / second_bias) + 1e-08)
            mbuf[n, rows, :] = master
            fbuf[n, rows, :] = first
            sbuf[n, rows, :] = second
        nm[:, cols] = mbuf[n, 0:BAND, :]
        nf[:, cols] = fbuf[n, 0:BAND, :]
        ns[:, cols] = sbuf[n, 0:BAND, :]

    for t in range(NT):
        wb[t] = jnp.concatenate(
            [nm[:, t * HALF : t * HALF + WIDE], nm[:, t * HALF + WIDE : (t + 1) * HALF]], axis=0
        ).astype(BF)


def run_b(pc, lo, rx, gq):
    smem = pl.BlockSpec(memory_space=pltpu.SMEM)
    vmem = pl.BlockSpec(memory_space=pltpu.VMEM)
    state = jax.ShapeDtypeStruct((BAND, 6144), F32)
    return pl.pallas_call(
        kernel_b,
        name="place_and_adam",
        out_shape=(state, state, state, jax.ShapeDtypeStruct((NT, 2 * BAND, WIDE), BF)),
        in_specs=[smem, smem, vmem, vmem],
        out_specs=(vmem, vmem, vmem, vmem),
        scratch_shapes=[
            pltpu.VMEM((4, 32 * SROWS + 32, 128), F32),
            pltpu.VMEM((12, 50, 8, 128), F32),
            pltpu.VMEM((48, 32, 128), F32),
            pltpu.VMEM((48, 32, 128), F32),
            pltpu.VMEM((48, 32, 128), F32),
            pltpu.VMEM((48, 32, 128), F32),
            pltpu.SMEM((128,), jnp.int32),
            pltpu.SemaphoreType.DMA((1,)),
        ],
        compiler_params=pltpu.CompilerParams(vmem_limit_bytes=40 * 2**20),
        cost_estimate=pl.CostEstimate(flops=10**9, bytes_accessed=5 * 2**20, transcendentals=0),
    )(pc, lo, rx, gq)


ZT = 5


def kernel_c(
    wb, nc, out, wg, wn, nv,
    nc_sem, own_sem, w1_s, w1_r, y1_s, y1_r, zz_s, zz_r, zy_s, zy_r, yz_s, yz_r,
):
    dp, t, y, z = where_am_i()
    load = pltpu.make_async_copy(nc, nv, nc_sem.at[0])
    load.start()
    own = pltpu.make_async_copy(wb.at[t], wg.at[y, z, t], own_sem.at[0])
    own.start()

    barrier = pltpu.get_barrier_semaphore()
    for k in range(1, NT):
        pl.semaphore_signal(barrier, inc=1, device_id=(dp, lax.rem(t + k, NT)), device_id_type=MESH)
    for k in range(1, NY):
        pl.semaphore_signal(
            barrier, inc=1, device_id=(lax.rem(y + k, NY) * NZ + z, t), device_id_type=MESH
        )
    for k in (1, NZ - 1):
        pl.semaphore_signal(
            barrier, inc=1, device_id=(y * NZ + lax.rem(z + k, NZ), t), device_id_type=MESH
        )
    pl.semaphore_wait(barrier, NT - 1 + NY - 1 + 2)

    def first_copy(k):
        to = lax.rem(t + k, NT)
        return remote(wb.at[to], wg.at[y, z, t], w1_s.at[k], w1_r.at[k], (dp, to))

    for k in range(1, NT):
        first_copy(k).start()
    own.wait()
    for k in range(1, NT):
        first_copy(k).wait()

    def over_y(k):
        piece = wg.at[y, z, pl.ds(ZT, NT - ZT)]
        return remote(piece, piece, y1_s.at[k], y1_r.at[k], (lax.rem(y + k, NY) * NZ + z, t))

    def around(d, s, part):
        sign = 1 if d == 0 else NZ - 1
        owner = lax.rem(z + (NZ - sign) * s, NZ)
        to = y * NZ + lax.rem(z + sign, NZ)
        if part == 0:
            piece = wg.at[y, owner, pl.ds(0, ZT)]
            return remote(piece, piece, zz_s.at[d, s], zz_r.at[d, s], (to, t))
        piece = wg.at[:, owner, pl.ds(ZT, NT - ZT)]
        return remote(piece, piece, yz_s.at[d, s], yz_r.at[d, s], (to, t))

    def steps(d, part):
        return 4 if d == part else 3

    def across(d, owner):
        sign = 1 if d == 0 else NY - 1
        piece = wg.at[y, owner, pl.ds(0, ZT)]
        return remote(
            piece, piece, zy_s.at[d, owner], zy_r.at[d, owner], (lax.rem(y + sign, NY) * NZ + z, t)
        )

    def onward(owner):
        odd = lax.rem(owner, 2)
        source = lax.rem(y + NY - 1 + 2 * odd, NY)
        target = lax.rem(y + 1 + 2 * odd, NY)
        piece = wg.at[source, owner, pl.ds(0, ZT)]
        return remote(piece, piece, zy_s.at[2, owner], zy_r.at[2, owner], (target * NZ + z, t))

    def spread(owner):
        across(0, owner).start()
        across(1, owner).start()

    def pass_on(owner):
        across(0, owner).wait_recv()
        across(1, owner).wait_recv()
        onward(owner).start()

    for k in (2, 1, 3):
        over_y(k).start()
    around(0, 0, 0).start()
    around(1, 0, 0).start()
    spread(z)
    for k in (1, 3, 2):
        over_y(k).wait_recv()
    around(0, 0, 1).start()
    around(1, 0, 1).start()

    done = [z]
    for s in range(1, 5):
        fresh = []
        for part in range(2):
            for d in range(2):
                if s - 1 < steps(d, part):
                    around(d, s - 1, part).wait_recv()
                    if s < steps(d, part):
                        around(d, s, part).start()
                    if part == 0:
                        sign = 1 if d == 0 else NZ - 1
                        owner = lax.rem(z + (NZ - sign) * s, NZ)
                        spread(owner)
                        fresh.append(owner)
        for owner in done:
            pass_on(owner)
        done = fresh
    for owner in done:
        pass_on(owner)

    @pl.loop(0, NZ)
    def _(owner):
        onward(owner).wait()
        across(0, owner).wait_send()
        across(1, owner).wait_send()

    for k in range(1, NY):
        over_y(k).wait_send()
    for d in range(2):
        for part in range(2):
            for s in range(steps(d, part)):
                around(d, s, part).wait_send()

    @pl.loop(0, NT)
    def _(tt):
        @pl.loop(0, 16)
        def _(pair):
            yy = pair // 4
            zz = lax.rem(pair, 4) * 2
            a = wg[yy, zz, tt].astype(F32)
            b = wg[yy, zz + 1, tt].astype(F32)
            rows = pl.ds(pl.multiple_of(pair * 48, 48), 48)
            wn[tt, rows, 0:WIDE] = jnp.concatenate([a[:BAND], b[:BAND]], axis=0).astype(BF)
            wn[tt, rows, WIDE:HALF] = jnp.concatenate([a[BAND:], b[BAND:]], axis=0).astype(BF)

    load.wait()

    @pl.loop(0, 3)
    def _(n):
        cols = pl.ds(pl.multiple_of(n * 256, 256), 256)
        total = jnp.dot(nv[0], wn[0, :, cols], preferred_element_type=F32)
        for tt in range(1, NT):
            total = total + jnp.dot(nv[tt], wn[tt, :, cols], preferred_element_type=F32)
        out[:, cols] = total.astype(BF)


def run_c(wb, nc):
    any_spec = pl.BlockSpec(memory_space=pl.ANY)
    vmem = pl.BlockSpec(memory_space=pltpu.VMEM)
    dma = pltpu.SemaphoreType.DMA
    return pl.pallas_call(
        kernel_c,
        name="weights_and_product",
        out_shape=jax.ShapeDtypeStruct((512, HALF), BF),
        in_specs=[vmem, any_spec],
        out_specs=vmem,
        scratch_shapes=[
            pltpu.VMEM((NY, NZ, NT, 2 * BAND, WIDE), BF),
            pltpu.VMEM((NT, HALF, HALF), BF),
            pltpu.VMEM((NT, 512, HALF), BF),
            dma((1,)), dma((1,)),
            dma((8,)), dma((8,)),
            dma((4,)), dma((4,)),
            dma((2, 4)), dma((2, 4)),
            dma((3, 8)), dma((3, 8)),
            dma((2, 4)), dma((2, 4)),
        ],
        compiler_params=pltpu.CompilerParams(
            collective_id=1, has_side_effects=True, vmem_limit_bytes=48 * 2**20
        ),
        cost_estimate=pl.CostEstimate(flops=2 * 512 * 6144 * 768, bytes_accessed=8 * 2**20, transcendentals=0),
    )(wb, nc)


def shards(
    saved_master,
    saved_first,
    saved_second,
    piece_columns,
    load_order,
    context,
    out_grad,
    next_context,
):
    def grouped(saved):
        return saved[0].reshape(4, 192, WIDE).transpose(1, 0, 2)

    tokens = lax.all_gather(next_context, "tensor")
    rx, gq = run_a(grouped(saved_master), grouped(saved_first), grouped(saved_second), context, out_grad)
    new_master, new_first, new_second, blocks = run_b(
        piece_columns[0], load_order[0], rx.reshape(32 * SROWS, WIDE), gq
    )
    activations = run_c(blocks, tokens)
    return (new_master, new_first, new_second, activations)


def solution(mesh):
    placed = (
        P("tensor", "dp", None),
        P("tensor", "dp", None),
        P("tensor", "dp", None),
        P("tensor", None),
        P("tensor", None),
        P("dp", "tensor"),
        P("dp", None),
        P("dp", "tensor"),
    )
    return jax.shard_map(
        shards,
        mesh=mesh,
        in_specs=placed,
        out_specs=(
            P(("tensor", "dp"), None),
            P(("tensor", "dp"), None),
            P(("tensor", "dp"), None),
            P("dp", "tensor"),
        ),
        check_vma=False,
    )
```

time: 531 us -> 220 us (0.41)
  waiting for transfers between devices: 274 us -> 0.7 us
  Pallas kernels: 0 us -> 199 us
  blocking collectives: 104 us -> 0 us
  local copies, waits for them, and re-layouts: 100 us -> 5.69 us
  matrix products: 20.7 us -> 0 us
  other arithmetic: 11.6 us -> 0 us
  starting transfers between devices: 6.59 us -> 0.04 us
    pallas_call x0 -> x3, Pallas kernels: none -> 199 us  [the longest x1 97.3 us: run_a(): pl.pallas_call(kernel_a, name='state_and_gradient', out_shape=(jax.ShapeD...]
    reduce_scatter x2 -> x0, waiting for transfers between devices: 142 us -> none  [the longest x1 73.4 us: shards(): lax.psum_scatter(partial_out, 'tensor', scatter_dimension=1, tiled=True)]
    all_to_all x2 -> x0, blocking collectives: 104 us -> none  [the longest x1 54.9 us: shards(): lax.all_to_all(send_first, 'dp', split_axis=1, concat_axis=0, tiled=True)]
    all_gather x1, waiting for transfers between devices: 101 us -> 0.02 us  [shards(): tokens = lax.all_gather(next_context, 'tensor')]
    gather x6 -> x0, local copies, waits for them, and re-layouts: 74.4 us -> none  [assemble(): return jnp.take(flat_rows, source, axis=1)]
    all_to_all x1 -> x0, waiting for transfers between devices: 30.3 us -> none  [shards(): lax.all_to_all(send_master, 'dp', split_axis=1, concat_axis=0, tiled=True)]
    dot_general x2 -> x0, matrix products: 20.7 us -> none  [the longest x1 11.9 us: shards(): jnp.dot(next_context, full_rows, preferred_element_type=jnp.float32)]
    transpose x3 -> x0, local copies, waits for them, and re-layouts: 13.1 us -> none  [assemble(): flat_rows = received.reshape(old_ranks, row_band, widest).transpose(1, 0,...]
  transfers between devices with their start and end apart: 4 -> 1, of which waited for: 4 -> 0; matrix products, arithmetic and copies ran while one was open for 19% -> 0% of each run, Pallas kernels for 0% -> 53%
where the time goes in v1:
time: 220 us
  Pallas kernels  199 us (90%)
  between operations  14.1 us (6%)
  local copies, waits for them, and re-layouts  5.69 us (3%)
    pallas_call x1, Pallas kernels, run_a(): pl.pallas_call(kernel_a, name='state_and_gradient', out_shape=(jax.ShapeD...  97.3 us
    pallas_call x1, Pallas kernels, run_c(): pl.pallas_call(kernel_c, name='weights_and_product', out_shape=jax.ShapeD...  83.1 us
    pallas_call x1, Pallas kernels, run_b(): pl.pallas_call(kernel_b, name='place_and_adam', out_shape=(state, state,...  18.6 us
    unnamed x13, local copies, waits for them, and re-layouts  5.69 us
  transfers between devices with their start and end apart: 1, of which 0 were waited for; matrix products, arithmetic and copies ran while one was open for 0% of the time, Pallas kernels for 53%

profile of v1, /device:TPU:8, one launch (start us, length us, event | category | flops | bytes accessed | tf_op | source)
XLA Modules:
  0.0 219.5 jit_solution(18402344939004897712)
XLA Ops:
  7.2 0.0 all-gather.3.cloned.1.call-start
  7.2 0.7 all-gather.3.cloned.1.call-update
  7.9 0.0 copy-start
  7.9 1.3 copy-done
  9.2 0.0 copy-start.1
  9.2 1.3 copy-done.1
  10.4 0.0 copy-start.2
  10.4 1.3 copy-done.2
  11.7 0.0 copy-start.3
  11.7 1.0 copy-done.3
  12.7 0.0 copy-start.4
  12.7 0.0 copy-start.5
  12.7 97.3 %state_and_gradient.1 = (bf16[32,80,384]{2,1,0:T(8,128)(2,1)S(1)}, bf16[4,2,48,384]{3,2,1,0:T(8,128)(2,1)S(1)}) custom-call(f32[192,4,384]{2,1,0:T(4,128)S(1)} %bitcast.13, f32[192,4,384]{2,1,0:T(4,128)S(1)} %bitcast.14, f32[192,4,384]{2,1,0:T(4,128)S(1)} %bitcast.15, bf16[256,768]{1,0:T(8,128)(2,1)S(1)} %copy-done.3, bf16[256,6144]{1,0:T(8,128)(2,1)} %og.1), custom_call_target="tpu_custom_call" | custom-call | flops 2415919104 | bytes 16777216 | tf_op jit(solution)/shard_map/state_and_gradient/pallas_call | solution.py:205
  110.1 0.0 copy-done.4
  110.1 0.0 copy-done.5
  110.1 18.6 %place_and_adam.1 = (f32[24,6144]{1,0:T(8,128)}, f32[24,6144]{1,0:T(8,128)}, f32[24,6144]{1,0:T(8,128)}, bf16[8,48,384]{2,1,0:T(8,128)(2,1)S(1)}) custom-call(s32[128]{0:T(128)S(1)} %bitcast.16, s32[128]{0:T(128)S(1)} %bitcast.17, bf16[2560,384]{1,0:T(8,128)(2,1)S(1)} %bitcast.18, bf16[4,2,48,384]{3,2,1,0:T(8,128)(2,1)S(1)} %get-tuple-element.11.gq), custom_call_target="tpu_custom_call" | custom-call | flops 1000000000 | bytes 5242880 | tf_op jit(solution)/shard_map/place_and_adam/pallas_call | solution.py:310
  128.6 0.0 all-gather.3.cloned.1.call-done
  128.7 83.1 %weights_and_product.1 = bf16[512,768]{1,0:T(8,128)(2,1)S(1)} custom-call(bf16[8,48,384]{2,1,0:T(8,128)(2,1)S(1)} %get-tuple-element.15.wb, bf16[8,512,768]{2,1,0:T(8,128)(2,1)} %bitcast.19), custom_call_target="tpu_custom_call" | custom-call | flops 4831838208 | bytes 8388608 | tf_op jit(solution)/shard_map/weights_and_product/pallas_call | solution.py:477
  211.8 0.9 copy.13
Async XLA Ops:
  7.2 121.5 %all-gather.3.cloned.1.call-start = ((), (), s32[]{:S(2)}) async-start(), calls=%async_computation | async-start | bytes 7077888 | tf_op jit(solution)/shard_map/all_gather | solution.py:514
  7.9 1.3 copy-start
  9.2 1.3 copy-start.1
  10.4 1.3 copy-start.2
  11.7 1.0 copy-start.3
  12.7 97.3 %copy-start.4 = (s32[1,128]{1,0:T(1,128)S(1)}, s32[1,128]{1,0:T(1,128)}, u32[]{:S(2)}) copy-start(s32[1,128]{1,0:T(1,128)} %param.11) | copy-start | bytes 1540
  12.7 97.4 %copy-start.5 = (s32[1,128]{1,0:T(1,128)S(1)}, s32[1,128]{1,0:T(1,128)}, u32[]{:S(2)}) copy-start(s32[1,128]{1,0:T(1,128)} %param.12) | copy-start | bytes 1540
Sparse Core Ops, SparseCore 0:
  9.8 46.3 all-gather.2

commit v2 on v1

--- a/solution.py
+++ b/solution.py
@@ -16,7 +16,7 @@
 BAND = 24
 WIDE = 384
 GROUPS = 6
-SROWS = 80
+SROWS = 72
 QUARTER = 1536
 HALF = 768
 
@@ -33,10 +33,13 @@
     )
 
 
+VMEM_A = 60 * 2**20
+
+
 def kernel_a(
     sm, sf, ss, ctx, og, rx, gq,
-    st, flat, tx, cg, ct, oq, grad, zs, zr, tot, ysb,
-    load_sem, loc_sem, st_s, st_r, cx_s, cx_r, og_s, og_r, fw_s, fw_r, rs_s, rs_r, ya_s, ya_r,
+    st, flat, tx, mid, ty, cg, ct, oq, grad, zs, zr, tot, ysb,
+    load_sem, loc_sem, st_s, st_r, sy_s, sy_r, cx_s, cx_r, og_s, og_r, fw_s, fw_r, rs_s, rs_r, ya_s, ya_r,
 ):
     dp, t, y, z = where_am_i()
     core = lax.rem(t, 2)
@@ -54,12 +57,16 @@
 
     barrier = pltpu.get_barrier_semaphore()
 
-    @pl.loop(1, 32)
-    def _(i):
-        pl.semaphore_signal(barrier, inc=1, device_id=(lax.rem(dp + i, 32), t), device_id_type=MESH)
-
+    for k in range(1, NY):
+        pl.semaphore_signal(
+            barrier, inc=1, device_id=(lax.rem(y + k, NY) * NZ + z, t), device_id_type=MESH
+        )
+    for k in range(1, NZ):
+        pl.semaphore_signal(
+            barrier, inc=1, device_id=(y * NZ + lax.rem(z + k, NZ), t), device_id_type=MESH
+        )
     pl.semaphore_signal(barrier, inc=1, device_id=(dp, mate), device_id_type=MESH)
-    pl.semaphore_wait(barrier, 32)
+    pl.semaphore_wait(barrier, NY - 1 + NZ - 1 + 1)
 
     def ctx_copy(k):
         to = lax.rem(y + k, NY)
@@ -84,27 +91,41 @@
     for copy in loads:
         copy.wait()
 
-    def state_copy(i):
-        to = lax.rem(y + i // NZ, NY) * NZ + lax.rem(z + lax.rem(i, NZ), NZ)
-        return to, remote(tx.at[to], rx.at[dp], st_s.at[i], st_r.at[i], (to, t))
-
-    def build(to):
-        for a in range(3):
-            for g in range(GROUPS):
-                flat[a * BAND + 4 * g : a * BAND + 4 * g + 4, :] = st[a, to * GROUPS + g]
-        tx[to] = flat[...].astype(BF)
-
-    flat[3 * BAND :, :] = jnp.zeros((SROWS - 3 * BAND, WIDE), F32)
-
-    @pl.loop(1, 32)
-    def _(i):
-        to, copy = state_copy(i)
-        build(to)
-        copy.start()
-
-    build(dp)
-    own_state = pltpu.make_async_copy(tx.at[dp], rx.at[dp], loc_sem.at[2])
-    own_state.start()
+    def state_copy(k):
+        to = lax.rem(z + k, NZ)
+        return remote(tx.at[k], mid.at[z], st_s.at[k], st_r.at[k], (y * NZ + to, t))
+
+    def build(k):
+        for ky in range(NY):
+            owner = lax.rem(y + ky, NY) * NZ + lax.rem(z + k, NZ)
+            for a in range(3):
+                for g in range(GROUPS):
+                    row = ky * SROWS + a * BAND + 4 * g
+                    flat[row : row + 4, :] = st[a, owner * GROUPS + g]
+        return flat[...].astype(BF)
+
+    for k in (4, 3, 5, 2, 6, 1, 7):
+        tx[k] = build(k)
+        state_copy(k).start()
+    mid[z] = build(0)
+
+    def state_over_y(k, pair):
+        to = lax.rem(y + k, NY) * NZ + z
+        return remote(ty.at[pair, k], rx.at[y * 4 + pair], sy_s.at[pair, k], sy_r.at[pair, k], (to, t))
+
+    def state_local(pair):
+        return pltpu.make_async_copy(ty.at[pair, 0], rx.at[y * 4 + pair], loc_sem.at[5 + pair])
+
+    def pass_state(pair):
+        low = mid[2 * pair].astype(F32)
+        high = mid[2 * pair + 1].astype(F32)
+        for k in (2, 1, 3, 0):
+            rows = slice(k * SROWS, (k + 1) * SROWS)
+            ty[pair, k] = jnp.concatenate([low[rows], high[rows]], axis=0).astype(BF)
+            if k:
+                state_over_y(k, pair).start()
+            else:
+                state_local(pair).start()
 
     own_ctx.wait()
     own_og.wait()
@@ -158,6 +179,11 @@
             for d in (h, 1 - h):
                 if s < steps(d, h):
                     ring_send(d, h, s)
+        if s == 1:
+            for k in (1, 7, 2, 6, 3, 5, 4):
+                state_copy(k).wait_recv()
+        for pair in ((0, 1), (2, 3), ())[s - 1]:
+            pass_state(pair)
 
     def out_copy(k, h):
         to = lax.rem(y + k, NY)
@@ -191,12 +217,12 @@
         for k in (1, 2, 3):
             out_copy(k, h).wait()
         own_out[h].wait()
-    own_state.wait()
-
-    @pl.loop(1, 32)
-    def _(i):
-        _, copy = state_copy(i)
-        copy.wait()
+    for k in range(1, NZ):
+        state_copy(k).wait_send()
+    for pair in range(4):
+        for k in (1, 2, 3):
+            state_over_y(k, pair).wait()
+        state_local(pair).wait()
 
 
 def run_a(sm, sf, ss, ctx, og):
@@ -206,15 +232,17 @@
         kernel_a,
         name="state_and_gradient",
         out_shape=(
-            jax.ShapeDtypeStruct((32, SROWS, WIDE), BF),
+            jax.ShapeDtypeStruct((16, 2 * SROWS, WIDE), BF),
             jax.ShapeDtypeStruct((NY, 2, 2 * BAND, WIDE), BF),
         ),
         in_specs=[any_spec] * 5,
         out_specs=(any_spec, any_spec),
         scratch_shapes=[
             pltpu.VMEM((3, 192, 4, WIDE), F32),
-            pltpu.VMEM((SROWS, WIDE), F32),
-            pltpu.VMEM((32, SROWS, WIDE), BF),
+            pltpu.VMEM((4 * SROWS, WIDE), F32),
+            pltpu.VMEM((NZ, 4 * SROWS, WIDE), BF),
+            pltpu.VMEM((NZ, 4 * SROWS, WIDE), BF),
+            pltpu.VMEM((4, NY, 2 * SROWS, WIDE), BF),
             pltpu.VMEM((1024, HALF), BF),
             pltpu.VMEM((HALF, 1024), BF),
             pltpu.VMEM((1024, QUARTER), BF),
@@ -223,20 +251,21 @@
             pltpu.VMEM((2, 2, 4, 4 * BAND, HALF), BF),
             pltpu.VMEM((4 * BAND, HALF), F32),
             pltpu.VMEM((4, 2, 2 * BAND, WIDE), BF),
-            dma((3,)), dma((5,)),
-            dma((32,)), dma((32,)),
+            dma((3,)), dma((9,)),
+            dma((8,)), dma((8,)),
+            dma((4, 4)), dma((4, 4)),
             dma((4,)), dma((4,)), dma((4,)), dma((4,)), dma((4,)), dma((4,)),
             dma((2, 2, 4)), dma((2, 2, 4)),
             dma((4, 2)), dma((4, 2)),
         ],
         compiler_params=pltpu.CompilerParams(
-            collective_id=0, has_side_effects=True, vmem_limit_bytes=48 * 2**20
+            collective_id=0, has_side_effects=True, vmem_limit_bytes=VMEM_A
         ),
         cost_estimate=pl.CostEstimate(flops=2 * 1024 * 768 * 1536, bytes_accessed=16 * 2**20, transcendentals=0),
     )(sm, sf, ss, ctx, og)
 
 
-def kernel_b(pc, lo, rx, gq, nm, nf, ns, wb, zbuf, obuf, gbuf, mbuf, fbuf, sbuf, starts, sem):
+def kernel_b(pc, lo, rx, gq, nm, nf, ns, wb, zbuf, obuf, gbuf, mbuf, fbuf, sbuf, starts):
     row = lax.broadcasted_iota(jnp.int32, (WIDE, 512), 0)
     col = lax.broadcasted_iota(jnp.int32, (WIDE, 512), 1)
     spread = ((row == (col // 128) * 96 + lax.rem(col, 128)) & (lax.rem(col, 128) < 96)).astype(BF)
@@ -247,7 +276,7 @@
 
     lax.fori_loop(0, 128, count, jnp.int32(0))
 
-    @pl.loop(0, 10)
+    @pl.loop(0, 9)
     def _(i):
         rows = pl.ds(i * 256, 256)
         value = jnp.dot(rx[rows, :], spread, preferred_element_type=F32)
@@ -264,7 +293,7 @@
 
     lane = lax.broadcasted_iota(jnp.int32, (8, 128), 1)
 
-    @pl.loop(0, 128)
+    @pl.loop(0, 128, unroll=4)
     def _(i):
         rank = lo[i]
         start = starts[rank]
@@ -281,7 +310,7 @@
                 pltpu.store(obuf.at[a * 4 + r, tile], value, mask=keep)
                 pltpu.store(obuf.at[a * 4 + r, tile + 1], value, mask=spill)
 
-    @pl.loop(0, 48)
+    @pl.loop(0, 48, unroll=4)
     def _(n):
         cols = pl.ds(pl.multiple_of(n * 128, 128), 128)
         for r in range(4):
@@ -321,7 +350,6 @@
             pltpu.VMEM((48, 32, 128), F32),
             pltpu.VMEM((48, 32, 128), F32),
             pltpu.SMEM((128,), jnp.int32),
-            pltpu.SemaphoreType.DMA((1,)),
         ],
         compiler_params=pltpu.CompilerParams(vmem_limit_bytes=40 * 2**20),
         cost_estimate=pl.CostEstimate(flops=10**9, bytes_accessed=5 * 2**20, transcendentals=0),

time: 220 us -> 192 us (0.87)
  Pallas kernels: 199 us -> 173 us
  local copies, waits for them, and re-layouts: 5.69 us -> 3.32 us
    pallas_call x1, Pallas kernels: 97.3 us -> 79.6 us  [run_a(): pl.pallas_call(kernel_a, name='state_and_gradient', out_shape=(jax.ShapeD...]
    pallas_call x1, Pallas kernels: 18.6 us -> 10.4 us  [run_b(): pl.pallas_call(kernel_b, name='place_and_adam', out_shape=(state, state,...]
    unnamed x13 -> x9, local copies, waits for them, and re-layouts: 5.69 us -> 3.32 us
  transfers between devices with their start and end apart: 1 -> 1, of which waited for: 0 -> 0; matrix products, arithmetic and copies ran while one was open for 0% -> 0% of each run, Pallas kernels for 53% -> 47%
where the time goes in v2:
time: 192 us
  Pallas kernels  173 us (90%)
  between operations  14.1 us (7%)
  local copies, waits for them, and re-layouts  3.32 us (2%)
    pallas_call x1, Pallas kernels, run_c(): pl.pallas_call(kernel_c, name='weights_and_product', out_shape=jax.ShapeD...  83.4 us
    pallas_call x1, Pallas kernels, run_a(): pl.pallas_call(kernel_a, name='state_and_gradient', out_shape=(jax.ShapeD...  79.6 us
    pallas_call x1, Pallas kernels, run_b(): pl.pallas_call(kernel_b, name='place_and_adam', out_shape=(state, state,...  10.4 us
  transfers between devices with their start and end apart: 1, of which 0 were waited for; matrix products, arithmetic and copies ran while one was open for 0% of the time, Pallas kernels for 47%

profile of v2, /device:TPU:8, one launch (start us, length us, event | category | flops | bytes accessed | tf_op | source)
XLA Modules:
  0.0 191.5 jit_solution(4063446679378154104)
XLA Ops:
  7.2 0.0 all-gather.3.cloned.1.call-start
  7.2 0.7 all-gather.3.cloned.1.call-update
  7.9 0.0 copy-start
  7.9 0.0 copy-start.1
  7.9 79.6 %state_and_gradient.1 = (bf16[16,144,384]{2,1,0:T(8,128)(2,1)}, bf16[4,2,48,384]{3,2,1,0:T(8,128)(2,1)}) custom-call(f32[192,4,384]{2,1,0:T(4,128)} %bitcast.17, f32[192,4,384]{2,1,0:T(4,128)} %bitcast.18, f32[192,4,384]{2,1,0:T(4,128)} %bitcast.19, bf16[256,768]{1,0:T(8,128)(2,1)} %ctx.1, bf16[256,6144]{1,0:T(8,128)(2,1)} %og.1), custom_call_target="tpu_custom_call" | custom-call | flops 2415919104 | bytes 16777216 | tf_op jit(solution)/shard_map/state_and_gradient/pallas_call | solution.py:231
  87.5 0.0 copy-done
  87.5 0.0 copy-done.1
  87.6 0.0 copy-start.2
  87.6 1.5 copy-done.2
  89.0 0.0 copy-start.3
  89.0 1.0 copy-done.3
  90.0 10.4 %place_and_adam.1 = (f32[24,6144]{1,0:T(8,128)}, f32[24,6144]{1,0:T(8,128)}, f32[24,6144]{1,0:T(8,128)}, bf16[8,48,384]{2,1,0:T(8,128)(2,1)S(1)}) custom-call(s32[128]{0:T(128)S(1)} %bitcast.13, s32[128]{0:T(128)S(1)} %bitcast.14, bf16[2304,384]{1,0:T(8,128)(2,1)S(1)} %bitcast.15, bf16[4,2,48,384]{3,2,1,0:T(8,128)(2,1)S(1)} %copy-done.3), custom_call_target="tpu_custom_call" | custom-call | flops 1000000000 | bytes 5242880 | tf_op jit(solution)/shard_map/place_and_adam/pallas_call | solution.py:339
  100.4 0.0 all-gather.3.cloned.1.call-done
  100.4 83.4 %weights_and_product.1 = bf16[512,768]{1,0:T(8,128)(2,1)S(1)} custom-call(bf16[8,48,384]{2,1,0:T(8,128)(2,1)S(1)} %get-tuple-element.15.wb, bf16[8,512,768]{2,1,0:T(8,128)(2,1)} %bitcast.16), custom_call_target="tpu_custom_call" | custom-call | flops 4831838208 | bytes 8388608 | tf_op jit(solution)/shard_map/weights_and_product/pallas_call | solution.py:505
  183.8 0.9 copy.13
Async XLA Ops:
  7.2 93.2 %all-gather.3.cloned.1.call-start = ((), (), s32[]{:S(2)}) async-start(), calls=%async_computation | async-start | bytes 7077888 | tf_op jit(solution)/shard_map/all_gather | solution.py:542
  7.9 79.6 %copy-start = (s32[1,128]{1,0:T(1,128)S(1)}, s32[1,128]{1,0:T(1,128)}, u32[]{:S(2)}) copy-start(s32[1,128]{1,0:T(1,128)} %param.11) | copy-start | bytes 1540
  7.9 79.6 %copy-start.1 = (s32[1,128]{1,0:T(1,128)S(1)}, s32[1,128]{1,0:T(1,128)}, u32[]{:S(2)}) copy-start(s32[1,128]{1,0:T(1,128)} %param.12) | copy-start | bytes 1540
  87.6 1.5 copy-start.2
  89.0 1.0 copy-start.3
Sparse Core Ops, SparseCore 0:
  9.8 46.3 all-gather.2

commit v3 on v2

--- a/solution.py
+++ b/solution.py
@@ -33,13 +33,17 @@
     )
 
 
+STAGGER = 2
+PARTS = 3
 VMEM_A = 60 * 2**20
+VMEM_C = 117 * 2**19
 
 
 def kernel_a(
-    sm, sf, ss, ctx, og, rx, gq,
-    st, flat, tx, mid, ty, cg, ct, oq, grad, zs, zr, tot, ysb,
-    load_sem, loc_sem, st_s, st_r, sy_s, sy_r, cx_s, cx_r, og_s, og_r, fw_s, fw_r, rs_s, rs_r, ya_s, ya_r,
+    sm, sf, ss, ctx, og, nc, rx, gq, nv,
+    st, flat, tx, mid, ty, cg, ct, oq, grad, zs, zr, tot, ysb, nraw, nsend,
+    load_sem, loc_sem, st_s, st_r, sy_s, sy_r, cx_s, cx_r, og_s, og_r, ox_s, ox_r, om_s, om_r, rs_s, rs_r, ya_s, ya_r,
+    ny_s, ny_r, nx_s, nx_r, nm_s, nm_r,
 ):
     dp, t, y, z = where_am_i()
     core = lax.rem(t, 2)
@@ -52,6 +56,8 @@
     own_og = pltpu.make_async_copy(
         og.at[:, pl.ds(y * QUARTER, QUARTER)], oq.at[pl.ds(y * 256, 256)], loc_sem.at[1]
     )
+    tokens_in = pltpu.make_async_copy(nc, nraw, loc_sem.at[9])
+    tokens_in.start()
     own_ctx.start()
     own_og.start()
 
@@ -65,8 +71,10 @@
         pl.semaphore_signal(
             barrier, inc=1, device_id=(y * NZ + lax.rem(z + k, NZ), t), device_id_type=MESH
         )
+    for k in range(1, 4):
+        pl.semaphore_signal(barrier, inc=1, device_id=(dp, lax.rem(t + 2 * k, NT)), device_id_type=MESH)
     pl.semaphore_signal(barrier, inc=1, device_id=(dp, mate), device_id_type=MESH)
-    pl.semaphore_wait(barrier, NY - 1 + NZ - 1 + 1)
+    pl.semaphore_wait(barrier, NY - 1 + NZ - 1 + 3 + 1)
 
     def ctx_copy(k):
         to = lax.rem(y + k, NY)
@@ -75,18 +83,53 @@
     def og_copy(k):
         to = lax.rem(y + k, NY)
         return remote(
-            og.at[pl.ds(core * 128, 128), pl.ds(to * QUARTER, QUARTER)],
-            oq.at[pl.ds(y * 256 + core * 128, 128)],
+            og.at[pl.ds(t * 32, 32), pl.ds(to * QUARTER, QUARTER)],
+            oq.at[pl.ds(y * 256 + t * 32, 32)],
             og_s.at[k], og_r.at[k], (to * NZ + z, t),
         )
 
-    def fw_copy(k):
-        rows = pl.ds(lax.rem(y + NY - k, NY) * 256 + core * 128, 128)
-        return remote(oq.at[rows], oq.at[rows], fw_s.at[k], fw_r.at[k], (dp, mate))
+    def og_rows(k, tt):
+        return oq.at[pl.ds(lax.rem(y + NY - k, NY) * 256 + tt * 32, 32)]
+
+    def og_over_x(k, kx):
+        piece = og_rows(k, t)
+        return remote(piece, piece, ox_s.at[k, kx], ox_r.at[k, kx], (dp, lax.rem(t + 2 * kx, NT)))
+
+    def og_to_mate(k, kx):
+        piece = og_rows(k, lax.rem(t + NT - 2 * kx, NT))
+        return remote(piece, piece, om_s.at[k, kx], om_r.at[k, kx], (dp, mate))
 
     for k in (2, 1, 3):
         og_copy(k).start()
         ctx_copy(k).start()
+
+    def lanes(tt):
+        return pl.ds(pl.multiple_of(tt * 128, 128), 128)
+
+    def tokens_over_y(k):
+        to = lax.rem(y + k, NY)
+        return remote(
+            nsend.at[to], nv.at[y, :, lanes(t)], ny_s.at[k], ny_r.at[k], (to * NZ + z, t)
+        )
+
+    def tokens_over_x(k):
+        piece = nv.at[:, :, lanes(t)]
+        return remote(piece, piece, nx_s.at[k], nx_r.at[k], (dp, lax.rem(t + 2 * k, NT)))
+
+    def tokens_to_mate(k):
+        piece = nv.at[:, :, lanes(lax.rem(t + NT - 2 * k, NT))]
+        return remote(piece, piece, nm_s.at[k], nm_r.at[k], (dp, mate))
+
+    own_tokens = pltpu.make_async_copy(nsend.at[y], nv.at[y, :, lanes(t)], loc_sem.at[10])
+    tokens_in.wait()
+    for yy in range(NY):
+        c0 = yy * 192
+        nsend[yy, 0:512, :] = nraw[:, c0 : c0 + 128]
+        tail = nraw[:, c0 + 128 : c0 + 192]
+        nsend[yy, 512:768, :] = jnp.concatenate([tail[:256], tail[256:]], axis=1)
+    for k in (2, 1, 3):
+        tokens_over_y(k).start()
+    own_tokens.start()
 
     for copy in loads:
         copy.wait()
@@ -127,6 +170,12 @@
             else:
                 state_local(pair).start()
 
+    for k in (1, 3, 2):
+        og_copy(k).wait_recv()
+        for kx in (2, 1, 3):
+            og_over_x(k, kx).start()
+        og_to_mate(k, 0).start()
+
     own_ctx.wait()
     own_og.wait()
 
@@ -134,14 +183,16 @@
         ct[:, pl.ds(source * 256, 256)] = cg[pl.ds(source * 256, 256), :].T
 
     turn(y)
-    for k in (1, 3, 2):
-        og_copy(k).wait_recv()
-        fw_copy(k).start()
     for k in (1, 3, 2):
         ctx_copy(k).wait_recv()
         turn(lax.rem(y + NY - k, NY))
     for k in (1, 3, 2):
-        fw_copy(k).wait_recv()
+        for kx in (1, 3, 2):
+            og_over_x(k, kx).wait_recv()
+            og_to_mate(k, kx).start()
+    for k in (1, 3, 2):
+        for kx in range(4):
+            og_to_mate(k, kx).wait_recv()
 
     def chunk(dest, h):
         return jnp.concatenate(
@@ -173,6 +224,13 @@
 
         ring_send(h, h, 0)
         ring_send(1 - h, h, 0)
+        if h == 0:
+            own_tokens.wait()
+            for k in (1, 3, 2):
+                tokens_over_y(k).wait_recv()
+            for k in (2, 1, 3):
+                tokens_over_x(k).start()
+            tokens_to_mate(0).start()
 
     for s in range(1, 4):
         for h in range(2):
@@ -184,6 +242,10 @@
                 state_copy(k).wait_recv()
         for pair in ((0, 1), (2, 3), ())[s - 1]:
             pass_state(pair)
+
+    for k in (1, 3, 2):
+        tokens_over_x(k).wait_recv()
+        tokens_to_mate(k).start()
 
     def out_copy(k, h):
         to = lax.rem(y + k, NY)
@@ -209,7 +271,10 @@
     for k in (1, 2, 3):
         og_copy(k).wait_send()
         ctx_copy(k).wait_send()
-        fw_copy(k).wait_send()
+        for kx in (1, 2, 3):
+            og_over_x(k, kx).wait_send()
+        for kx in range(4):
+            og_to_mate(k, kx).wait_send()
     for h in range(2):
         for d in range(2):
             for s in range(steps(d, h)):
@@ -219,14 +284,19 @@
         own_out[h].wait()
     for k in range(1, NZ):
         state_copy(k).wait_send()
+    for k in range(1, 4):
+        tokens_over_y(k).wait_send()
+        tokens_over_x(k).wait_send()
+    for k in range(4):
+        tokens_to_mate(k).wait()
     for pair in range(4):
         for k in (1, 2, 3):
             state_over_y(k, pair).wait()
         state_local(pair).wait()
 
 
-def run_a(sm, sf, ss, ctx, og):
-    any_spec = pl.BlockSpec(memory_space=pl.ANY)
+def run_a(sm, sf, ss, ctx, og, nc):
+    hbm = pl.BlockSpec(memory_space=pltpu.HBM)
     dma = pltpu.SemaphoreType.DMA
     return pl.pallas_call(
         kernel_a,
@@ -234,9 +304,10 @@
         out_shape=(
             jax.ShapeDtypeStruct((16, 2 * SROWS, WIDE), BF),
             jax.ShapeDtypeStruct((NY, 2, 2 * BAND, WIDE), BF),
+            jax.ShapeDtypeStruct((NY, 768, 1024), BF),
         ),
-        in_specs=[any_spec] * 5,
-        out_specs=(any_spec, any_spec),
+        in_specs=[hbm] * 6,
+        out_specs=(hbm, hbm, hbm),
         scratch_shapes=[
             pltpu.VMEM((3, 192, 4, WIDE), F32),
             pltpu.VMEM((4 * SROWS, WIDE), F32),
@@ -251,21 +322,29 @@
             pltpu.VMEM((2, 2, 4, 4 * BAND, HALF), BF),
             pltpu.VMEM((4 * BAND, HALF), F32),
             pltpu.VMEM((4, 2, 2 * BAND, WIDE), BF),
-            dma((3,)), dma((9,)),
+            pltpu.VMEM((512, HALF), BF),
+            pltpu.VMEM((NY, 768, 128), BF),
+            dma((3,)), dma((11,)),
             dma((8,)), dma((8,)),
             dma((4, 4)), dma((4, 4)),
-            dma((4,)), dma((4,)), dma((4,)), dma((4,)), dma((4,)), dma((4,)),
+            dma((4,)), dma((4,)), dma((4,)), dma((4,)),
+            dma((4, 4)), dma((4, 4)), dma((4, 4)), dma((4, 4)),
             dma((2, 2, 4)), dma((2, 2, 4)),
             dma((4, 2)), dma((4, 2)),
+            dma((4,)), dma((4,)), dma((4,)), dma((4,)), dma((4,)), dma((4,)),
         ],
         compiler_params=pltpu.CompilerParams(
             collective_id=0, has_side_effects=True, vmem_limit_bytes=VMEM_A
         ),
         cost_estimate=pl.CostEstimate(flops=2 * 1024 * 768 * 1536, bytes_accessed=16 * 2**20, transcendentals=0),
-    )(sm, sf, ss, ctx, og)
-
-
-def kernel_b(pc, lo, rx, gq, nm, nf, ns, wb, zbuf, obuf, gbuf, mbuf, fbuf, sbuf, starts):
+    )(sm, sf, ss, ctx, og, nc)
+
+
+def kernel_b(pc, lo, rx_in, gq_in, nm, nf, ns, wb, rx, gq, sem, zbuf, obuf, gbuf, mbuf, fbuf, sbuf, starts):
+    gq_copy = pltpu.make_async_copy(gq_in, gq, sem.at[0])
+    rx_copy = pltpu.make_async_copy(rx_in, rx, sem.at[1])
+    gq_copy.start()
+    rx_copy.start()
     row = lax.broadcasted_iota(jnp.int32, (WIDE, 512), 0)
     col = lax.broadcasted_iota(jnp.int32, (WIDE, 512), 1)
     spread = ((row == (col // 128) * 96 + lax.rem(col, 128)) & (lax.rem(col, 128) < 96)).astype(BF)
@@ -276,13 +355,7 @@
 
     lax.fori_loop(0, 128, count, jnp.int32(0))
 
-    @pl.loop(0, 9)
-    def _(i):
-        rows = pl.ds(i * 256, 256)
-        value = jnp.dot(rx[rows, :], spread, preferred_element_type=F32)
-        for r in range(4):
-            zbuf[r, rows, :] = value[:, r * 128 : (r + 1) * 128]
-
+    gq_copy.wait()
     for yy in range(NY):
         for h in range(2):
             block = gq[yy, h].astype(F32)
@@ -290,6 +363,15 @@
                 c0 = yy * QUARTER + h * HALF + q * WIDE
                 for n in range(3):
                     gbuf[c0 // 128 + n, 0:BAND, :] = block[q * BAND : (q + 1) * BAND, n * 128 : (n + 1) * 128]
+
+    rx_copy.wait()
+
+    @pl.loop(0, 9)
+    def _(i):
+        rows = pl.ds(i * 256, 256)
+        value = jnp.dot(rx[rows, :], spread, preferred_element_type=F32)
+        for r in range(4):
+            zbuf[r, rows, :] = value[:, r * 128 : (r + 1) * 128]
 
     lane = lax.broadcasted_iota(jnp.int32, (8, 128), 1)
 
@@ -326,23 +408,27 @@
         nf[:, cols] = fbuf[n, 0:BAND, :]
         ns[:, cols] = sbuf[n, 0:BAND, :]
 
-    for t in range(NT):
-        wb[t] = jnp.concatenate(
-            [nm[:, t * HALF : t * HALF + WIDE], nm[:, t * HALF + WIDE : (t + 1) * HALF]], axis=0
-        ).astype(BF)
+    for n in range(PARTS):
+        for t in range(NT):
+            c0 = t * HALF + n * 256
+            wb[n, t] = jnp.concatenate([nm[:, c0 : c0 + 128], nm[:, c0 + 128 : c0 + 256]], axis=0).astype(BF)
 
 
 def run_b(pc, lo, rx, gq):
     smem = pl.BlockSpec(memory_space=pltpu.SMEM)
     vmem = pl.BlockSpec(memory_space=pltpu.VMEM)
+    hbm = pl.BlockSpec(memory_space=pltpu.HBM)
     state = jax.ShapeDtypeStruct((BAND, 6144), F32)
     return pl.pallas_call(
         kernel_b,
         name="place_and_adam",
-        out_shape=(state, state, state, jax.ShapeDtypeStruct((NT, 2 * BAND, WIDE), BF)),
-        in_specs=[smem, smem, vmem, vmem],
+        out_shape=(state, state, state, jax.ShapeDtypeStruct((PARTS, NT, 2 * BAND, 128), BF)),
+        in_specs=[smem, smem, hbm, hbm],
         out_specs=(vmem, vmem, vmem, vmem),
         scratch_shapes=[
+            pltpu.VMEM((32 * SROWS, WIDE), BF),
+            pltpu.VMEM((NY, 2, 2 * BAND, WIDE), BF),
+            pltpu.SemaphoreType.DMA((2,)),
             pltpu.VMEM((4, 32 * SROWS + 32, 128), F32),
             pltpu.VMEM((12, 50, 8, 128), F32),
             pltpu.VMEM((48, 32, 128), F32),
@@ -351,23 +437,20 @@
             pltpu.VMEM((48, 32, 128), F32),
             pltpu.SMEM((128,), jnp.int32),
         ],
-        compiler_params=pltpu.CompilerParams(vmem_limit_bytes=40 * 2**20),
+        compiler_params=pltpu.CompilerParams(vmem_limit_bytes=VMEM_A),
         cost_estimate=pl.CostEstimate(flops=10**9, bytes_accessed=5 * 2**20, transcendentals=0),
     )(pc, lo, rx, gq)
 
 
-ZT = 5
-
-
 def kernel_c(
-    wb, nc, out, wg, wn, nv,
-    nc_sem, own_sem, w1_s, w1_r, y1_s, y1_r, zz_s, zz_r, zy_s, zy_r, yz_s, yz_r,
+    wb, nc, out, wg, wa, wl, wh, nv, own, po, ro,
+    nc_sem, own_sem, w1_s, w1_r, zz_s, zz_r, yo_s, yo_r,
 ):
     dp, t, y, z = where_am_i()
     load = pltpu.make_async_copy(nc, nv, nc_sem.at[0])
     load.start()
-    own = pltpu.make_async_copy(wb.at[t], wg.at[y, z, t], own_sem.at[0])
-    own.start()
+    own_in = pltpu.make_async_copy(wb.at[:, t], wg.at[:, z, t], own_sem.at[0])
+    own_in.start()
 
     barrier = pltpu.get_barrier_semaphore()
     for k in range(1, NT):
@@ -384,143 +467,122 @@
 
     def first_copy(k):
         to = lax.rem(t + k, NT)
-        return remote(wb.at[to], wg.at[y, z, t], w1_s.at[k], w1_r.at[k], (dp, to))
+        return remote(wb.at[:, to], wg.at[:, z, t], w1_s.at[k], w1_r.at[k], (dp, to))
 
     for k in range(1, NT):
         first_copy(k).start()
-    own.wait()
+    wl[...] = jnp.zeros_like(wl)
+    wh[...] = jnp.zeros_like(wh)
+    own_in.wait()
     for k in range(1, NT):
         first_copy(k).wait()
 
-    def over_y(k):
-        piece = wg.at[y, z, pl.ds(ZT, NT - ZT)]
-        return remote(piece, piece, y1_s.at[k], y1_r.at[k], (lax.rem(y + k, NY) * NZ + z, t))
-
-    def around(d, s, part):
+    def steps(d, n):
+        return 4 if d == n % 2 else 3
+
+    def around(d, s, n):
         sign = 1 if d == 0 else NZ - 1
         owner = lax.rem(z + (NZ - sign) * s, NZ)
-        to = y * NZ + lax.rem(z + sign, NZ)
-        if part == 0:
-            piece = wg.at[y, owner, pl.ds(0, ZT)]
-            return remote(piece, piece, zz_s.at[d, s], zz_r.at[d, s], (to, t))
-        piece = wg.at[:, owner, pl.ds(ZT, NT - ZT)]
-        return remote(piece, piece, yz_s.at[d, s], yz_r.at[d, s], (to, t))
-
-    def steps(d, part):
-        return 4 if d == part else 3
-
-    def across(d, owner):
-        sign = 1 if d == 0 else NY - 1
-        piece = wg.at[y, owner, pl.ds(0, ZT)]
+        piece = wg.at[n, owner]
         return remote(
-            piece, piece, zy_s.at[d, owner], zy_r.at[d, owner], (lax.rem(y + sign, NY) * NZ + z, t)
-        )
-
-    def onward(owner):
-        odd = lax.rem(owner, 2)
-        source = lax.rem(y + NY - 1 + 2 * odd, NY)
-        target = lax.rem(y + 1 + 2 * odd, NY)
-        piece = wg.at[source, owner, pl.ds(0, ZT)]
-        return remote(piece, piece, zy_s.at[2, owner], zy_r.at[2, owner], (target * NZ + z, t))
-
-    def spread(owner):
-        across(0, owner).start()
-        across(1, owner).start()
-
-    def pass_on(owner):
-        across(0, owner).wait_recv()
-        across(1, owner).wait_recv()
-        onward(owner).start()
-
-    for k in (2, 1, 3):
-        over_y(k).start()
-    around(0, 0, 0).start()
-    around(1, 0, 0).start()
-    spread(z)
-    for k in (1, 3, 2):
-        over_y(k).wait_recv()
-    around(0, 0, 1).start()
-    around(1, 0, 1).start()
-
-    done = [z]
-    for s in range(1, 5):
-        fresh = []
-        for part in range(2):
+            piece, piece, zz_s.at[d, s, n], zz_r.at[d, s, n], (y * NZ + lax.rem(z + sign, NZ), t)
+        )
+
+    def back(k, n):
+        to = lax.rem(y + k, NY) * NZ + z
+        return remote(po.at[n, k - 1], ro.at[n, k - 1], yo_s.at[k, n], yo_r.at[k, n], (to, t))
+
+    def arrange(n):
+        @pl.loop(0, NT)
+        def _(tt):
+            base = pl.multiple_of(tt * 128, 128)
+            for pair in range(4):
+                a = wg[n, 2 * pair, tt].astype(F32)
+                b = wg[n, 2 * pair + 1, tt].astype(F32)
+                for q in range(2):
+                    rows = slice(q * BAND, (q + 1) * BAND)
+                    cols = slice(q * 128, (q + 1) * 128)
+                    both = jnp.concatenate([a[rows], b[rows]], axis=0).astype(BF)
+                    if pair < 2:
+                        wa[n, pl.ds(base + pair * 48, 48), cols] = both
+                    elif pair == 2:
+                        wa[n, pl.ds(base + 96, 32), cols] = both[:32]
+                        wl[n, pl.ds(base, 16), cols] = both[32:]
+                        wh[n, pl.ds(base + 64, 16), cols] = both[32:]
+                    else:
+                        wl[n, pl.ds(base + 16, 48), cols] = both
+                        wh[n, pl.ds(base + 80, 48), cols] = both
+
+    def multiply(n):
+        for k in (2, 1, 3, 0):
+            ys = lax.rem(y + k, NY)
+            for half, tail in ((0, wl), (1, wh)):
+                rows = slice(half * 256, (half + 1) * 256)
+                value = jnp.dot(nv[ys, rows, :], wa[n], preferred_element_type=F32)
+                value = value + jnp.dot(nv[ys, 512:768, :], tail[n], preferred_element_type=F32)
+                if k:
+                    po[n, k - 1, rows, :] = value.astype(BF)
+                else:
+                    own[n, rows, :] = value
+            if k:
+                back(k, n).start()
+
+    for tick in range(5 + STAGGER * (PARTS - 1)):
+        for n in range(PARTS):
+            s = tick - STAGGER * n
             for d in range(2):
-                if s - 1 < steps(d, part):
-                    around(d, s - 1, part).wait_recv()
-                    if s < steps(d, part):
-                        around(d, s, part).start()
-                    if part == 0:
-                        sign = 1 if d == 0 else NZ - 1
-                        owner = lax.rem(z + (NZ - sign) * s, NZ)
-                        spread(owner)
-                        fresh.append(owner)
-        for owner in done:
-            pass_on(owner)
-        done = fresh
-    for owner in done:
-        pass_on(owner)
-
-    @pl.loop(0, NZ)
-    def _(owner):
-        onward(owner).wait()
-        across(0, owner).wait_send()
-        across(1, owner).wait_send()
-
-    for k in range(1, NY):
-        over_y(k).wait_send()
-    for d in range(2):
-        for part in range(2):
-            for s in range(steps(d, part)):
-                around(d, s, part).wait_send()
-
-    @pl.loop(0, NT)
-    def _(tt):
-        @pl.loop(0, 16)
-        def _(pair):
-            yy = pair // 4
-            zz = lax.rem(pair, 4) * 2
-            a = wg[yy, zz, tt].astype(F32)
-            b = wg[yy, zz + 1, tt].astype(F32)
-            rows = pl.ds(pl.multiple_of(pair * 48, 48), 48)
-            wn[tt, rows, 0:WIDE] = jnp.concatenate([a[:BAND], b[:BAND]], axis=0).astype(BF)
-            wn[tt, rows, WIDE:HALF] = jnp.concatenate([a[BAND:], b[BAND:]], axis=0).astype(BF)
-
-    load.wait()
-
-    @pl.loop(0, 3)
-    def _(n):
-        cols = pl.ds(pl.multiple_of(n * 256, 256), 256)
-        total = jnp.dot(nv[0], wn[0, :, cols], preferred_element_type=F32)
-        for tt in range(1, NT):
-            total = total + jnp.dot(nv[tt], wn[tt, :, cols], preferred_element_type=F32)
-        out[:, cols] = total.astype(BF)
+                if s > 0 and s - 1 < steps(d, n):
+                    around(d, s - 1, n).wait_recv()
+                if 0 <= s < steps(d, n):
+                    around(d, s, n).start()
+        for n in range(PARTS):
+            if tick - STAGGER * n == 4:
+                if n == 0:
+                    load.wait()
+                arrange(n)
+                multiply(n)
+
+    for n in range(PARTS):
+        value = own[n]
+        for k in (1, 3, 2):
+            back(k, n).wait_recv()
+            value = value + ro[n, k - 1].astype(F32)
+        out[:, n * 256 : (n + 1) * 256] = value.astype(BF)
+
+    for n in range(PARTS):
+        for d in range(2):
+            for s in range(steps(d, n)):
+                around(d, s, n).wait_send()
+        for k in range(1, NY):
+            back(k, n).wait_send()
 
 
 def run_c(wb, nc):
-    any_spec = pl.BlockSpec(memory_space=pl.ANY)
+    hbm = pl.BlockSpec(memory_space=pltpu.HBM)
     vmem = pl.BlockSpec(memory_space=pltpu.VMEM)
     dma = pltpu.SemaphoreType.DMA
     return pl.pallas_call(
         kernel_c,
         name="weights_and_product",
         out_shape=jax.ShapeDtypeStruct((512, HALF), BF),
-        in_specs=[vmem, any_spec],
+        in_specs=[hbm, hbm],
         out_specs=vmem,
         scratch_shapes=[
-            pltpu.VMEM((NY, NZ, NT, 2 * BAND, WIDE), BF),
-            pltpu.VMEM((NT, HALF, HALF), BF),
-            pltpu.VMEM((NT, 512, HALF), BF),
+            pltpu.VMEM((PARTS, NZ, NT, 2 * BAND, 128), BF),
+            pltpu.VMEM((PARTS, 1024, 256), BF),
+            pltpu.VMEM((PARTS, 1024, 256), BF),
+            pltpu.VMEM((PARTS, 1024, 256), BF),
+            pltpu.VMEM((NY, 768, 1024), BF),
+            pltpu.VMEM((PARTS, 512, 256), F32),
+            pltpu.VMEM((PARTS, NY - 1, 512, 256), BF),
+            pltpu.VMEM((PARTS, NY - 1, 512, 256), BF),
             dma((1,)), dma((1,)),
             dma((8,)), dma((8,)),
-            dma((4,)), dma((4,)),
-            dma((2, 4)), dma((2, 4)),
-            dma((3, 8)), dma((3, 8)),
-            dma((2, 4)), dma((2, 4)),
+            dma((2, 4, PARTS)), dma((2, 4, PARTS)),
+            dma((4, PARTS)), dma((4, PARTS)),
         ],
         compiler_params=pltpu.CompilerParams(
-            collective_id=1, has_side_effects=True, vmem_limit_bytes=48 * 2**20
+            collective_id=1, has_side_effects=True, vmem_limit_bytes=VMEM_C
         ),
         cost_estimate=pl.CostEstimate(flops=2 * 512 * 6144 * 768, bytes_accessed=8 * 2**20, transcendentals=0),
     )(wb, nc)
@@ -539,8 +601,9 @@
     def grouped(saved):
         return saved[0].reshape(4, 192, WIDE).transpose(1, 0, 2)
 
-    tokens = lax.all_gather(next_context, "tensor")
-    rx, gq = run_a(grouped(saved_master), grouped(saved_first), grouped(saved_second), context, out_grad)
+    rx, gq, tokens = run_a(
+        grouped(saved_master), grouped(saved_first), grouped(saved_second), context, out_grad, next_context
+    )
     new_master, new_first, new_second, blocks = run_b(
         piece_columns[0], load_order[0], rx.reshape(32 * SROWS, WIDE), gq
     )

time: 192 us -> 164 us (0.85)
  between operations: 14.1 us -> 0.66 us
  Pallas kernels: 173 us -> 160 us
    pallas_call x1, Pallas kernels: 83.4 us -> 62.8 us  [run_c(): pl.pallas_call(kernel_c, name='weights_and_product', out_shape=jax.ShapeD...]
    pallas_call x1, Pallas kernels: 79.6 us -> 85.6 us  [run_a(): pl.pallas_call(kernel_a, name='state_and_gradient', out_shape=(jax.ShapeD...]
  transfers between devices with their start and end apart: 1 -> 0, of which waited for: 0 -> 0; matrix products, arithmetic and copies ran while one was open for 0% -> 0% of each run, Pallas kernels for 47% -> 0%
where the time goes in v3:
time: 164 us; the launch traced here: 162 us
  Pallas kernels  160 us (98%)
  local copies, waits for them, and re-layouts  2.06 us (1%)
    pallas_call x1, Pallas kernels, run_a(): pl.pallas_call(kernel_a, name='state_and_gradient', out_shape=(jax.ShapeD...  85.6 us
    pallas_call x1, Pallas kernels, run_c(): pl.pallas_call(kernel_c, name='weights_and_product', out_shape=jax.ShapeD...  62.8 us
    pallas_call x1, Pallas kernels, run_b(): pl.pallas_call(kernel_b, name='place_and_adam', out_shape=(state, state,...  11.3 us

profile of v3, /device:TPU:8, one launch (start us, length us, event | category | flops | bytes accessed | tf_op | source)
XLA Modules:
  0.0 162.4 jit_solution(14818887343714321548)
XLA Ops:
  0.6 85.6 %state_and_gradient.1 = (bf16[16,144,384]{2,1,0:T(8,128)(2,1)}, bf16[4,2,48,384]{3,2,1,0:T(8,128)(2,1)}, bf16[4,768,1024]{2,1,0:T(8,128)(2,1)}) custom-call(f32[192,4,384]{2,1,0:T(4,128)} %bitcast.12, f32[192,4,384]{2,1,0:T(4,128)} %bitcast.13, f32[192,4,384]{2,1,0:T(4,128)} %bitcast.14, bf16[256,768]{1,0:T(8,128)(2,1)} %ctx.1, bf16[256,6144]{1,0:T(8,128)(2,1)} %og.1, ...), custom_call_target="tpu_custom_call" | custom-call | flops 2415919104 | bytes 16777216 | tf_op jit(solution)/shard_map/state_and_gradient/pallas_call | solution.py:301
  86.2 11.3 %place_and_adam.1 = (f32[24,6144]{1,0:T(8,128)}, f32[24,6144]{1,0:T(8,128)}, f32[24,6144]{1,0:T(8,128)}, bf16[3,8,48,128]{3,2,1,0:T(8,128)(2,1)}) custom-call(s32[128]{0:T(128)} %bitcast.15, s32[128]{0:T(128)} %bitcast.16, bf16[2304,384]{1,0:T(8,128)(2,1)} %bitcast.17, bf16[4,2,48,384]{3,2,1,0:T(8,128)(2,1)} %get-tuple-element.12.gq_in), custom_call_target="tpu_custom_call" | custom-call | flops 1000000000 | bytes 5242880 | tf_op jit(solution)/shard_map/place_and_adam/pallas_call | solution.py:422
  97.5 62.8 %weights_and_product.1 = bf16[512,768]{1,0:T(8,128)(2,1)} custom-call(bf16[3,8,48,128]{3,2,1,0:T(8,128)(2,1)} %get-tuple-element.16.wb, bf16[4,768,1024]{2,1,0:T(8,128)(2,1)} %get-tuple-element.17.nc), custom_call_target="tpu_custom_call" | custom-call | flops 4831838208 | bytes 8388608 | tf_op jit(solution)/shard_map/weights_and_product/pallas_call | solution.py:564
  160.3 2.1 %copy.13 = bf16[512,768]{1,0:T(8,128)(2,1)} copy(bf16[512,768]{1,0:T(8,128)(2,1)} %weights_and_product.1) | data formatting | bytes 1572864

commit v4 on v3

--- a/solution.py
+++ b/solution.py
@@ -36,7 +36,8 @@
 STAGGER = 2
 PARTS = 3
 VMEM_A = 60 * 2**20
-VMEM_C = 117 * 2**19
+VMEM_C = 104 * 2**19
+VMEM_B = 125 * 2**19
 
 
 def kernel_a(
@@ -437,13 +438,13 @@
             pltpu.VMEM((48, 32, 128), F32),
             pltpu.SMEM((128,), jnp.int32),
         ],
-        compiler_params=pltpu.CompilerParams(vmem_limit_bytes=VMEM_A),
+        compiler_params=pltpu.CompilerParams(vmem_limit_bytes=VMEM_B),
         cost_estimate=pl.CostEstimate(flops=10**9, bytes_accessed=5 * 2**20, transcendentals=0),
     )(pc, lo, rx, gq)
 
 
 def kernel_c(
-    wb, nc, out, wg, wa, wl, wh, nv, own, po, ro,
+    wb, nc, out, wg, wa, wl, wh, nv, own, held, po, ro,
     nc_sem, own_sem, w1_s, w1_r, zz_s, zz_r, yo_s, yo_r,
 ):
     dp, t, y, z = where_am_i()
@@ -465,32 +466,32 @@
         )
     pl.semaphore_wait(barrier, NT - 1 + NY - 1 + 2)
 
-    def first_copy(k):
+    def first_copy(k, n):
         to = lax.rem(t + k, NT)
-        return remote(wb.at[:, to], wg.at[:, z, t], w1_s.at[k], w1_r.at[k], (dp, to))
-
-    for k in range(1, NT):
-        first_copy(k).start()
+        return remote(wb.at[n, to], wg.at[n, z, t], w1_s.at[k, n], w1_r.at[k, n], (dp, to))
+
+    for n in range(PARTS):
+        for k in range(1, NT):
+            first_copy(k, n).start()
     wl[...] = jnp.zeros_like(wl)
     wh[...] = jnp.zeros_like(wh)
     own_in.wait()
-    for k in range(1, NT):
-        first_copy(k).wait()
 
     def steps(d, n):
         return 4 if d == n % 2 else 3
 
-    def around(d, s, n):
+    def around(d, s, n, part):
         sign = 1 if d == 0 else NZ - 1
         owner = lax.rem(z + (NZ - sign) * s, NZ)
-        piece = wg.at[n, owner]
+        piece = wg.at[n, owner, pl.ds(part * 4, 4)]
         return remote(
-            piece, piece, zz_s.at[d, s, n], zz_r.at[d, s, n], (y * NZ + lax.rem(z + sign, NZ), t)
-        )
-
-    def back(k, n):
-        to = lax.rem(y + k, NY) * NZ + z
-        return remote(po.at[n, k - 1], ro.at[n, k - 1], yo_s.at[k, n], yo_r.at[k, n], (to, t))
+            piece, piece, zz_s.at[d, s, n, part], zz_r.at[d, s, n, part],
+            (y * NZ + lax.rem(z + sign, NZ), t),
+        )
+
+    def back(kind, n):
+        to = lax.rem(y + (1 if kind % 2 == 0 else NY - 1), NY) * NZ + z
+        return remote(po.at[n, kind], ro.at[n, kind], yo_s.at[kind, n], yo_r.at[kind, n], (to, t))
 
     def arrange(n):
         @pl.loop(0, NT)
@@ -513,48 +514,67 @@
                         wl[n, pl.ds(base + 16, 48), cols] = both
                         wh[n, pl.ds(base + 80, 48), cols] = both
 
+    def product(n, k, half):
+        ys = lax.rem(y + k, NY)
+        value = jnp.dot(nv[ys, half * 256 : half * 256 + 256, :], wa[n], preferred_element_type=F32)
+        tail = (wl, wh)[half]
+        return value + jnp.dot(nv[ys, 512:768, :], tail[n], preferred_element_type=F32)
+
     def multiply(n):
-        for k in (2, 1, 3, 0):
-            ys = lax.rem(y + k, NY)
-            for half, tail in ((0, wl), (1, wh)):
-                rows = slice(half * 256, (half + 1) * 256)
-                value = jnp.dot(nv[ys, rows, :], wa[n], preferred_element_type=F32)
-                value = value + jnp.dot(nv[ys, 512:768, :], tail[n], preferred_element_type=F32)
-                if k:
-                    po[n, k - 1, rows, :] = value.astype(BF)
-                else:
-                    own[n, rows, :] = value
-            if k:
-                back(k, n).start()
-
-    for tick in range(5 + STAGGER * (PARTS - 1)):
+        for kind, k, half in ((0, 2, 0), (1, 2, 1), (2, 1, 1), (3, 3, 0)):
+            po[n, kind] = product(n, k, half).astype(BF)
+            back(kind, n).start()
+        held[n, 0] = product(n, 1, 0)
+        held[n, 1] = product(n, 3, 1)
+        own[n, 0:256, :] = product(n, 0, 0)
+        own[n, 256:512, :] = product(n, 0, 1)
+
+    def join(n):
+        for d in range(2):
+            back(d, n).wait_recv()
+            po[n, 4 + d] = (held[n, d] + ro[n, d].astype(F32)).astype(BF)
+            back(4 + d, n).start()
+
+    for tick in range(6 + STAGGER * (PARTS - 1)):
         for n in range(PARTS):
             s = tick - STAGGER * n
-            for d in range(2):
-                if s > 0 and s - 1 < steps(d, n):
-                    around(d, s - 1, n).wait_recv()
-                if 0 <= s < steps(d, n):
-                    around(d, s, n).start()
+            if s == 0:
+                for k in range(1, NT):
+                    first_copy(k, n).wait_recv()
+            for part in range(2):
+                for d in range(2):
+                    if s > 0 and s - 1 < steps(d, n):
+                        around(d, s - 1, n, part).wait_recv()
+                    if 0 <= s < steps(d, n):
+                        around(d, s, n, part).start()
         for n in range(PARTS):
             if tick - STAGGER * n == 4:
                 if n == 0:
                     load.wait()
                 arrange(n)
                 multiply(n)
+            if tick - STAGGER * n == 5:
+                join(n)
 
     for n in range(PARTS):
-        value = own[n]
-        for k in (1, 3, 2):
-            back(k, n).wait_recv()
-            value = value + ro[n, k - 1].astype(F32)
-        out[:, n * 256 : (n + 1) * 256] = value.astype(BF)
+        cols = slice(n * 256, (n + 1) * 256)
+        for half, kinds in ((0, (3, 4)), (1, (2, 5))):
+            rows = slice(half * 256, half * 256 + 256)
+            value = own[n, rows, :]
+            for kind in kinds:
+                back(kind, n).wait_recv()
+                value = value + ro[n, kind].astype(F32)
+            out[rows, cols] = value.astype(BF)
 
     for n in range(PARTS):
+        for k in range(1, NT):
+            first_copy(k, n).wait_send()
         for d in range(2):
             for s in range(steps(d, n)):
-                around(d, s, n).wait_send()
-        for k in range(1, NY):
-            back(k, n).wait_send()
+                for part in range(2):
+                    around(d, s, n, part).wait_send()
+        for kind in range(6):
+            back(kind, n).wait_send()
 
 
 def run_c(wb, nc):
@@ -574,12 +594,13 @@
             pltpu.VMEM((PARTS, 1024, 256), BF),
             pltpu.VMEM((NY, 768, 1024), BF),
             pltpu.VMEM((PARTS, 512, 256), F32),
-            pltpu.VMEM((PARTS, NY - 1, 512, 256), BF),
-            pltpu.VMEM((PARTS, NY - 1, 512, 256), BF),
+            pltpu.VMEM((PARTS, 2, 256, 256), F32),
+            pltpu.VMEM((PARTS, 6, 256, 256), BF),
+            pltpu.VMEM((PARTS, 6, 256, 256), BF),
             dma((1,)), dma((1,)),
-            dma((8,)), dma((8,)),
-            dma((2, 4, PARTS)), dma((2, 4, PARTS)),
-            dma((4, PARTS)), dma((4, PARTS)),
+            dma((8, PARTS)), dma((8, PARTS)),
+            dma((2, 4, PARTS, 2)), dma((2, 4, PARTS, 2)),
+            dma((6, PARTS)), dma((6, PARTS)),
         ],
         compiler_params=pltpu.CompilerParams(
             collective_id=1, has_side_effects=True, vmem_limit_bytes=VMEM_C

time: 164 us -> 155 us (0.945)
  Pallas kernels: 160 us -> 152 us
    pallas_call x1, Pallas kernels: 62.8 us -> 55.3 us  [run_c(): pl.pallas_call(kernel_c, name='weights_and_product', out_shape=jax.ShapeD...]
where the time goes in v4:
time: 155 us
  Pallas kernels  152 us (98%)
  local copies, waits for them, and re-layouts  1.84 us (1%)
    pallas_call x1, Pallas kernels, run_a(): pl.pallas_call(kernel_a, name='state_and_gradient', out_shape=(jax.ShapeD...  85.6 us
    pallas_call x1, Pallas kernels, run_c(): pl.pallas_call(kernel_c, name='weights_and_product', out_shape=jax.ShapeD...  55.3 us
    pallas_call x1, Pallas kernels, run_b(): pl.pallas_call(kernel_b, name='place_and_adam', out_shape=(state, state,...  11.3 us

profile of v4, /device:TPU:8, one launch (start us, length us, event | category | flops | bytes accessed | tf_op | source)
XLA Modules:
  0.0 154.7 jit_solution(241902719209116641)
XLA Ops:
  0.6 85.6 %state_and_gradient.1 = (bf16[16,144,384]{2,1,0:T(8,128)(2,1)}, bf16[4,2,48,384]{3,2,1,0:T(8,128)(2,1)}, bf16[4,768,1024]{2,1,0:T(8,128)(2,1)}) custom-call(f32[192,4,384]{2,1,0:T(4,128)} %bitcast.12, f32[192,4,384]{2,1,0:T(4,128)} %bitcast.13, f32[192,4,384]{2,1,0:T(4,128)} %bitcast.14, bf16[256,768]{1,0:T(8,128)(2,1)} %ctx.1, bf16[256,6144]{1,0:T(8,128)(2,1)} %og.1, ...), custom_call_target="tpu_custom_call" | custom-call | flops 2415919104 | bytes 16777216 | tf_op jit(solution)/shard_map/state_and_gradient/pallas_call | solution.py:302
  86.2 11.3 %place_and_adam.1 = (f32[24,6144]{1,0:T(8,128)}, f32[24,6144]{1,0:T(8,128)}, f32[24,6144]{1,0:T(8,128)}, bf16[3,8,48,128]{3,2,1,0:T(8,128)(2,1)}) custom-call(s32[128]{0:T(128)} %bitcast.15, s32[128]{0:T(128)} %bitcast.16, bf16[2304,384]{1,0:T(8,128)(2,1)} %bitcast.17, bf16[4,2,48,384]{3,2,1,0:T(8,128)(2,1)} %get-tuple-element.12.gq_in), custom_call_target="tpu_custom_call" | custom-call | flops 1000000000 | bytes 5242880 | tf_op jit(solution)/shard_map/place_and_adam/pallas_call | solution.py:423
  97.5 0.0 copy-start
  97.5 1.0 copy-done
  98.5 55.3 %weights_and_product.1 = bf16[512,768]{1,0:T(8,128)(2,1)S(1)} custom-call(bf16[3,8,48,128]{3,2,1,0:T(8,128)(2,1)S(1)} %copy-done, bf16[4,768,1024]{2,1,0:T(8,128)(2,1)} %get-tuple-element.17.nc), custom_call_target="tpu_custom_call" | custom-call | flops 4831838208 | bytes 8388608 | tf_op jit(solution)/shard_map/weights_and_product/pallas_call | solution.py:584
  153.8 0.9 copy.13
Async XLA Ops:
  97.5 1.0 copy-start

commit v5 on v4

--- a/solution.py
+++ b/solution.py
@@ -33,11 +33,13 @@
     )
 
 
+SUBS = (4, 2, 2)
 STAGGER = 2
+ROOM = 32
 PARTS = 3
 VMEM_A = 60 * 2**20
 VMEM_C = 104 * 2**19
-VMEM_B = 125 * 2**19
+VMEM_B = 60 * 2**20
 
 
 def kernel_a(
@@ -100,10 +102,6 @@
         piece = og_rows(k, lax.rem(t + NT - 2 * kx, NT))
         return remote(piece, piece, om_s.at[k, kx], om_r.at[k, kx], (dp, mate))
 
-    for k in (2, 1, 3):
-        og_copy(k).start()
-        ctx_copy(k).start()
-
     def lanes(tt):
         return pl.ds(pl.multiple_of(tt * 128, 128), 128)
 
@@ -121,6 +119,8 @@
         piece = nv.at[:, :, lanes(lax.rem(t + NT - 2 * k, NT))]
         return remote(piece, piece, nm_s.at[k], nm_r.at[k], (dp, mate))
 
+    for k in (2, 1, 3):
+        og_copy(k).start()
     own_tokens = pltpu.make_async_copy(nsend.at[y], nv.at[y, :, lanes(t)], loc_sem.at[10])
     tokens_in.wait()
     for yy in range(NY):
@@ -131,13 +131,15 @@
     for k in (2, 1, 3):
         tokens_over_y(k).start()
     own_tokens.start()
+    for k in (2, 1, 3):
+        ctx_copy(k).start()
 
     for copy in loads:
         copy.wait()
 
     def state_copy(k):
         to = lax.rem(z + k, NZ)
-        return remote(tx.at[k], mid.at[z], st_s.at[k], st_r.at[k], (y * NZ + to, t))
+        return remote(tx.at[k], mid.at[k], st_s.at[k], st_r.at[k], (y * NZ + to, t))
 
     def build(k):
         for ky in range(NY):
@@ -151,7 +153,7 @@
     for k in (4, 3, 5, 2, 6, 1, 7):
         tx[k] = build(k)
         state_copy(k).start()
-    mid[z] = build(0)
+    mid[0] = build(0)
 
     def state_over_y(k, pair):
         to = lax.rem(y + k, NY) * NZ + z
@@ -161,8 +163,12 @@
         return pltpu.make_async_copy(ty.at[pair, 0], rx.at[y * 4 + pair], loc_sem.at[5 + pair])
 
     def pass_state(pair):
-        low = mid[2 * pair].astype(F32)
-        high = mid[2 * pair + 1].astype(F32)
+        first, second = ((0, 4), (3, 5), (2, 6), (1, 7))[pair]
+        if first:
+            state_copy(first).wait_recv()
+        state_copy(second).wait_recv()
+        low = mid[first].astype(F32)
+        high = mid[second].astype(F32)
         for k in (2, 1, 3, 0):
             rows = slice(k * SROWS, (k + 1) * SROWS)
             ty[pair, k] = jnp.concatenate([low[rows], high[rows]], axis=0).astype(BF)
@@ -176,6 +182,12 @@
         for kx in (2, 1, 3):
             og_over_x(k, kx).start()
         og_to_mate(k, 0).start()
+    own_tokens.wait()
+    for k in (1, 3, 2):
+        tokens_over_y(k).wait_recv()
+    for k in (2, 1, 3):
+        tokens_over_x(k).start()
+    tokens_to_mate(0).start()
 
     own_ctx.wait()
     own_og.wait()
@@ -225,23 +237,14 @@
 
         ring_send(h, h, 0)
         ring_send(1 - h, h, 0)
-        if h == 0:
-            own_tokens.wait()
-            for k in (1, 3, 2):
-                tokens_over_y(k).wait_recv()
-            for k in (2, 1, 3):
-                tokens_over_x(k).start()
-            tokens_to_mate(0).start()
-
+
+    pass_state(0)
     for s in range(1, 4):
         for h in range(2):
             for d in (h, 1 - h):
                 if s < steps(d, h):
                     ring_send(d, h, s)
-        if s == 1:
-            for k in (1, 7, 2, 6, 3, 5, 4):
-                state_copy(k).wait_recv()
-        for pair in ((0, 1), (2, 3), ())[s - 1]:
+        for pair in ((1, 2), (3,), ())[s - 1]:
             pass_state(pair)
 
     for k in (1, 3, 2):
@@ -341,19 +344,29 @@
     )(sm, sf, ss, ctx, og, nc)
 
 
-def kernel_b(pc, lo, rx_in, gq_in, nm, nf, ns, wb, rx, gq, sem, zbuf, obuf, gbuf, mbuf, fbuf, sbuf, starts):
+def kernel_b(pc_in, lo_in, rx_in, gq_in, nm, nf, ns, wb_out, pc, lo, wb, rx, gq, vm, vf, vs, sem, out_sem, zbuf, obuf, gbuf, mbuf, fbuf, sbuf, starts):
     gq_copy = pltpu.make_async_copy(gq_in, gq, sem.at[0])
-    rx_copy = pltpu.make_async_copy(rx_in, rx, sem.at[1])
+    rx_copies = [
+        pltpu.make_async_copy(rx_in.at[pl.ds(i * 576, 576)], rx.at[pl.ds(i * 576, 576)], sem.at[1 + i])
+        for i in range(4)
+    ]
+    small = [
+        pltpu.make_async_copy(src, dst, sem.at[5 + i]) for i, (src, dst) in enumerate(((pc_in, pc), (lo_in, lo)))
+    ]
+    for copy in small:
+        copy.start()
     gq_copy.start()
-    rx_copy.start()
-    row = lax.broadcasted_iota(jnp.int32, (WIDE, 512), 0)
-    col = lax.broadcasted_iota(jnp.int32, (WIDE, 512), 1)
-    spread = ((row == (col // 128) * 96 + lax.rem(col, 128)) & (lax.rem(col, 128) < 96)).astype(BF)
+    for copy in rx_copies:
+        copy.start()
+
+    z = lax.rem(lax.axis_index("dp"), NZ)
 
     def count(j, total):
         starts[j] = total
         return total + pc[j]
 
+    for copy in small:
+        copy.wait()
     lax.fori_loop(0, 128, count, jnp.int32(0))
 
     gq_copy.wait()
@@ -365,18 +378,19 @@
                 for n in range(3):
                     gbuf[c0 // 128 + n, 0:BAND, :] = block[q * BAND : (q + 1) * BAND, n * 128 : (n + 1) * 128]
 
-    rx_copy.wait()
-
-    @pl.loop(0, 9)
-    def _(i):
-        rows = pl.ds(i * 256, 256)
-        value = jnp.dot(rx[rows, :], spread, preferred_element_type=F32)
-        for r in range(4):
-            zbuf[r, rows, :] = value[:, r * 128 : (r + 1) * 128]
+    for i in range(4):
+        rx_copies[i].wait()
+
+        @pl.loop(i * 4, i * 4 + 4, unroll=2)
+        def _(i):
+            rows = pl.ds(i * 144, 144)
+            value = rx[rows, :].astype(F32)
+            for tile in range(3):
+                zbuf[tile, rows, :] = value[:, tile * 128 : (tile + 1) * 128]
 
     lane = lax.broadcasted_iota(jnp.int32, (8, 128), 1)
 
-    @pl.loop(0, 128, unroll=4)
+    @pl.loop(0, 128, unroll=8)
     def _(i):
         rank = lo[i]
         start = starts[rank]
@@ -385,52 +399,80 @@
         offset = lax.rem(start, 128)
         keep = (lane >= offset) & (lane < offset + length)
         spill = lane < offset + length - 128
-        base = (i // 4) * SROWS + lax.rem(i, 4)
+        k = lax.rem(z + NZ - lax.rem(i // 4, NZ), NZ)
+        far = k // 4
+        pair = lax.rem(NY + (2 * far - 1) * k, NY)
+        slot = (i // 32) * NZ + 2 * pair + far
+        base = slot * SROWS + lax.rem(i, 4)
         for a in range(3):
-            for r in range(4):
-                value = zbuf[r, pl.ds(base + a * BAND, 8, stride=4), :]
-                value = pltpu.roll(value, offset, 1)
+            low, middle, high = (zbuf[tile, pl.ds(base + a * BAND, 8, stride=4), :] for tile in range(3))
+            for r, value in enumerate(
+                (low, jnp.where(lane >= 96, low, middle), jnp.where(lane >= 64, middle, high), high)
+            ):
+                value = pltpu.roll(value, lax.rem(offset + 32 * r, 128), 1)
                 pltpu.store(obuf.at[a * 4 + r, tile], value, mask=keep)
                 pltpu.store(obuf.at[a * 4 + r, tile + 1], value, mask=spill)
 
-    @pl.loop(0, 48, unroll=4)
-    def _(n):
-        cols = pl.ds(pl.multiple_of(n * 128, 128), 128)
-        for r in range(4):
-            rows = pl.ds(r, 8, stride=4)
-            gradient = gbuf[n, rows, :]
-            first = 0.9 * obuf[4 + r, n] + 0.1 * gradient
-            second = 0.95 * obuf[8 + r, n] + 0.05 * gradient * gradient
-            master = obuf[r, n] - 0.01 * (first / first_bias) / (jnp.sqrt(second / second_bias) + 1e-08)
-            mbuf[n, rows, :] = master
-            fbuf[n, rows, :] = first
-            sbuf[n, rows, :] = second
-        nm[:, cols] = mbuf[n, 0:BAND, :]
-        nf[:, cols] = fbuf[n, 0:BAND, :]
-        ns[:, cols] = sbuf[n, 0:BAND, :]
-
-    for n in range(PARTS):
-        for t in range(NT):
-            c0 = t * HALF + n * 256
-            wb[n, t] = jnp.concatenate([nm[:, c0 : c0 + 128], nm[:, c0 + 128 : c0 + 256]], axis=0).astype(BF)
+    def results(t):
+        cols = pl.ds(pl.multiple_of(t * HALF, HALF), HALF)
+        return [
+            pltpu.make_async_copy(src.at[:, cols], dst.at[:, cols], out_sem.at[a, t])
+            for a, (src, dst) in enumerate(((vm, nm), (vf, nf), (vs, ns)))
+        ]
+
+    @pl.loop(0, NT)
+    def _(t):
+        for c in range(6):
+            n = t * 6 + c
+            cols = pl.ds(pl.multiple_of(n * 128, 128), 128)
+            for r in range(4):
+                rows = pl.ds(r, 8, stride=4)
+                gradient = gbuf[n, rows, :]
+                first = 0.9 * obuf[4 + r, n] + 0.1 * gradient
+                second = 0.95 * obuf[8 + r, n] + 0.05 * gradient * gradient
+                master = obuf[r, n] - 0.01 * (first / first_bias) / (jnp.sqrt(second / second_bias) + 1e-08)
+                mbuf[n, rows, :] = master
+                fbuf[n, rows, :] = first
+                sbuf[n, rows, :] = second
+            vm[:, cols] = mbuf[n, 0:BAND, :]
+            vf[:, cols] = fbuf[n, 0:BAND, :]
+            vs[:, cols] = sbuf[n, 0:BAND, :]
+        for copy in results(t):
+            copy.start()
+        for part in range(PARTS):
+            wb[part, t] = jnp.concatenate(
+                [mbuf[t * 6 + 2 * part, 0:BAND, :], mbuf[t * 6 + 2 * part + 1, 0:BAND, :]], axis=0
+            ).astype(BF)
+
+    weights = pltpu.make_async_copy(wb, wb_out.at[pl.ds(0, PARTS)], sem.at[7])
+    weights.start()
+    for t in range(NT):
+        for copy in results(t):
+            copy.wait()
+    weights.wait()
 
 
 def run_b(pc, lo, rx, gq):
-    smem = pl.BlockSpec(memory_space=pltpu.SMEM)
-    vmem = pl.BlockSpec(memory_space=pltpu.VMEM)
     hbm = pl.BlockSpec(memory_space=pltpu.HBM)
     state = jax.ShapeDtypeStruct((BAND, 6144), F32)
     return pl.pallas_call(
         kernel_b,
         name="place_and_adam",
-        out_shape=(state, state, state, jax.ShapeDtypeStruct((PARTS, NT, 2 * BAND, 128), BF)),
-        in_specs=[smem, smem, hbm, hbm],
-        out_specs=(vmem, vmem, vmem, vmem),
+        out_shape=(state, state, state, jax.ShapeDtypeStruct((ROOM, NT, 2 * BAND, 128), BF)),
+        in_specs=[hbm, hbm, hbm, hbm],
+        out_specs=(hbm, hbm, hbm, hbm),
         scratch_shapes=[
+            pltpu.SMEM((128,), jnp.int32),
+            pltpu.SMEM((128,), jnp.int32),
+            pltpu.VMEM((PARTS, NT, 2 * BAND, 128), BF),
             pltpu.VMEM((32 * SROWS, WIDE), BF),
             pltpu.VMEM((NY, 2, 2 * BAND, WIDE), BF),
-            pltpu.SemaphoreType.DMA((2,)),
-            pltpu.VMEM((4, 32 * SROWS + 32, 128), F32),
+            pltpu.VMEM((BAND, 6144), F32),
+            pltpu.VMEM((BAND, 6144), F32),
+            pltpu.VMEM((BAND, 6144), F32),
+            pltpu.SemaphoreType.DMA((8,)),
+            pltpu.SemaphoreType.DMA((3, NT)),
+            pltpu.VMEM((3, 32 * SROWS + 32, 128), F32),
             pltpu.VMEM((12, 50, 8, 128), F32),
             pltpu.VMEM((48, 32, 128), F32),
             pltpu.VMEM((48, 32, 128), F32),
@@ -450,7 +492,7 @@
     dp, t, y, z = where_am_i()
     load = pltpu.make_async_copy(nc, nv, nc_sem.at[0])
     load.start()
-    own_in = pltpu.make_async_copy(wb.at[:, t], wg.at[:, z, t], own_sem.at[0])
+    own_in = pltpu.make_async_copy(wb.at[pl.ds(0, PARTS), t], wg.at[:, z, t], own_sem.at[0])
     own_in.start()
 
     barrier = pltpu.get_barrier_semaphore()
@@ -477,13 +519,14 @@
     wh[...] = jnp.zeros_like(wh)
     own_in.wait()
 
-    def steps(d, n):
-        return 4 if d == n % 2 else 3
+    def steps(d, part):
+        return 4 if d == part % 2 else 3
 
     def around(d, s, n, part):
         sign = 1 if d == 0 else NZ - 1
         owner = lax.rem(z + (NZ - sign) * s, NZ)
-        piece = wg.at[n, owner, pl.ds(part * 4, 4)]
+        width = NT // SUBS[n]
+        piece = wg.at[n, owner, pl.ds(part * width, width)]
         return remote(
             piece, piece, zz_s.at[d, s, n, part], zz_r.at[d, s, n, part],
             (y * NZ + lax.rem(z + sign, NZ), t),
@@ -541,11 +584,11 @@
             if s == 0:
                 for k in range(1, NT):
                     first_copy(k, n).wait_recv()
-            for part in range(2):
+            for part in range(SUBS[n]):
                 for d in range(2):
-                    if s > 0 and s - 1 < steps(d, n):
+                    if s > 0 and s - 1 < steps(d, part):
                         around(d, s - 1, n, part).wait_recv()
-                    if 0 <= s < steps(d, n):
+                    if 0 <= s < steps(d, part):
                         around(d, s, n, part).start()
         for n in range(PARTS):
             if tick - STAGGER * n == 4:
@@ -570,8 +613,8 @@
         for k in range(1, NT):
             first_copy(k, n).wait_send()
         for d in range(2):
-            for s in range(steps(d, n)):
-                for part in range(2):
+            for part in range(SUBS[n]):
+                for s in range(steps(d, part)):
                     around(d, s, n, part).wait_send()
         for kind in range(6):
             back(kind, n).wait_send()
@@ -599,7 +642,7 @@
             pltpu.VMEM((PARTS, 6, 256, 256), BF),
             dma((1,)), dma((1,)),
             dma((8, PARTS)), dma((8, PARTS)),
-            dma((2, 4, PARTS, 2)), dma((2, 4, PARTS, 2)),
+            dma((2, 4, PARTS, 4)), dma((2, 4, PARTS, 4)),
             dma((6, PARTS)), dma((6, PARTS)),
         ],
         compiler_params=pltpu.CompilerParams(

time: 155 us -> 149 us (0.961)
  Pallas kernels: 152 us -> 147 us
    pallas_call x1, Pallas kernels: 85.6 us -> 81.9 us  [run_a(): pl.pallas_call(kernel_a, name='state_and_gradient', out_shape=(jax.ShapeD...]
    pallas_call x1, Pallas kernels: 11.3 us -> 9.27 us  [run_b(): pl.pallas_call(kernel_b, name='place_and_adam', out_shape=(state, state,...]
where the time goes in v5:
time: 149 us
  Pallas kernels  147 us (99%)
    pallas_call x1, Pallas kernels, run_a(): pl.pallas_call(kernel_a, name='state_and_gradient', out_shape=(jax.ShapeD...  81.9 us
    pallas_call x1, Pallas kernels, run_c(): pl.pallas_call(kernel_c, name='weights_and_product', out_shape=jax.ShapeD...  55.9 us
    pallas_call x1, Pallas kernels, run_b(): pl.pallas_call(kernel_b, name='place_and_adam', out_shape=(state, state,...  9.27 us

profile of v5, /device:TPU:8, one launch (start us, length us, event | category | flops | bytes accessed | tf_op | source)
XLA Modules:
  0.0 148.6 jit_solution(14547562878792719698)
XLA Ops:
  0.6 81.9 %state_and_gradient.1 = (bf16[16,144,384]{2,1,0:T(8,128)(2,1)}, bf16[4,2,48,384]{3,2,1,0:T(8,128)(2,1)}, bf16[4,768,1024]{2,1,0:T(8,128)(2,1)}) custom-call(f32[192,4,384]{2,1,0:T(4,128)} %bitcast.12, f32[192,4,384]{2,1,0:T(4,128)} %bitcast.13, f32[192,4,384]{2,1,0:T(4,128)} %bitcast.14, bf16[256,768]{1,0:T(8,128)(2,1)} %ctx.1, bf16[256,6144]{1,0:T(8,128)(2,1)} %og.1, ...), custom_call_target="tpu_custom_call" | custom-call | flops 2415919104 | bytes 16777216 | tf_op jit(solution)/shard_map/state_and_gradient/pallas_call | solution.py:305
  82.5 9.3 %place_and_adam.1 = (f32[24,6144]{1,0:T(8,128)}, f32[24,6144]{1,0:T(8,128)}, f32[24,6144]{1,0:T(8,128)}, bf16[32,8,48,128]{3,2,1,0:T(8,128)(2,1)}) custom-call(s32[128]{0:T(128)} %bitcast.15, s32[128]{0:T(128)} %bitcast.16, bf16[2304,384]{1,0:T(8,128)(2,1)} %bitcast.17, bf16[4,2,48,384]{3,2,1,0:T(8,128)(2,1)} %get-tuple-element.12.gq_in), custom_call_target="tpu_custom_call" | custom-call | flops 1000000000 | bytes 5242880 | tf_op jit(solution)/shard_map/place_and_adam/pallas_call | solution.py:458
  91.8 55.9 %weights_and_product.1 = bf16[512,768]{1,0:T(8,128)(2,1)S(1)} custom-call(bf16[32,8,48,128]{3,2,1,0:T(8,128)(2,1)} %get-tuple-element.16.wb, bf16[4,768,1024]{2,1,0:T(8,128)(2,1)} %get-tuple-element.17.nc), custom_call_target="tpu_custom_call" | custom-call | flops 4831838208 | bytes 8388608 | tf_op jit(solution)/shard_map/weights_and_product/pallas_call | solution.py:627
  147.7 0.9 copy.13

commit v6 on v5

--- a/solution.py
+++ b/solution.py
@@ -111,13 +111,27 @@
             nsend.at[to], nv.at[y, :, lanes(t)], ny_s.at[k], ny_r.at[k], (to * NZ + z, t)
         )
 
-    def tokens_over_x(k):
-        piece = nv.at[:, :, lanes(t)]
-        return remote(piece, piece, nx_s.at[k], nx_r.at[k], (dp, lax.rem(t + 2 * k, NT)))
-
-    def tokens_to_mate(k):
-        piece = nv.at[:, :, lanes(lax.rem(t + NT - 2 * k, NT))]
-        return remote(piece, piece, nm_s.at[k], nm_r.at[k], (dp, mate))
+    def tokens_over_x(k, kx):
+        piece = nv.at[lax.rem(y + NY - k, NY), :, lanes(t)]
+        return remote(
+            piece if k else nsend.at[y], piece, nx_s.at[k, kx], nx_r.at[k, kx], (dp, lax.rem(t + 2 * kx, NT))
+        )
+
+    def tokens_to_mate(k, kx):
+        piece = nv.at[lax.rem(y + NY - k, NY), :, lanes(lax.rem(t + NT - 2 * kx, NT))]
+        return remote(
+            piece if k or kx else nsend.at[y], piece, nm_s.at[k, kx], nm_r.at[k, kx], (dp, mate)
+        )
+
+    def tokens_onward(k):
+        for kx in (2, 1, 3):
+            tokens_over_x(k, kx).start()
+        tokens_to_mate(k, 0).start()
+
+    def tokens_passed(k):
+        for kx in (1, 3, 2):
+            tokens_over_x(k, kx).wait_recv()
+            tokens_to_mate(k, kx).start()
 
     for k in (2, 1, 3):
         og_copy(k).start()
@@ -131,6 +145,7 @@
     for k in (2, 1, 3):
         tokens_over_y(k).start()
     own_tokens.start()
+    tokens_onward(0)
     for k in (2, 1, 3):
         ctx_copy(k).start()
 
@@ -182,12 +197,9 @@
         for kx in (2, 1, 3):
             og_over_x(k, kx).start()
         og_to_mate(k, 0).start()
-    own_tokens.wait()
     for k in (1, 3, 2):
         tokens_over_y(k).wait_recv()
-    for k in (2, 1, 3):
-        tokens_over_x(k).start()
-    tokens_to_mate(0).start()
+        tokens_onward(k)
 
     own_ctx.wait()
     own_og.wait()
@@ -239,6 +251,7 @@
         ring_send(1 - h, h, 0)
 
     pass_state(0)
+    tokens_passed(0)
     for s in range(1, 4):
         for h in range(2):
             for d in (h, 1 - h):
@@ -246,10 +259,10 @@
                     ring_send(d, h, s)
         for pair in ((1, 2), (3,), ())[s - 1]:
             pass_state(pair)
-
-    for k in (1, 3, 2):
-        tokens_over_x(k).wait_recv()
-        tokens_to_mate(k).start()
+        for k in ((), (1,), (3,))[s - 1]:
+            tokens_passed(k)
+
+    tokens_passed(2)
 
     def out_copy(k, h):
         to = lax.rem(y + k, NY)
@@ -290,9 +303,12 @@
         state_copy(k).wait_send()
     for k in range(1, 4):
         tokens_over_y(k).wait_send()
-        tokens_over_x(k).wait_send()
+    own_tokens.wait()
     for k in range(4):
-        tokens_to_mate(k).wait()
+        for kx in range(1, 4):
+            tokens_over_x(k, kx).wait_send()
+        for kx in range(4):
+            tokens_to_mate(k, kx).wait()
     for pair in range(4):
         for k in (1, 2, 3):
             state_over_y(k, pair).wait()
@@ -335,7 +351,7 @@
             dma((4, 4)), dma((4, 4)), dma((4, 4)), dma((4, 4)),
             dma((2, 2, 4)), dma((2, 2, 4)),
             dma((4, 2)), dma((4, 2)),
-            dma((4,)), dma((4,)), dma((4,)), dma((4,)), dma((4,)), dma((4,)),
+            dma((4,)), dma((4,)), dma((4, 4)), dma((4, 4)), dma((4, 4)), dma((4, 4)),
         ],
         compiler_params=pltpu.CompilerParams(
             collective_id=0, has_side_effects=True, vmem_limit_bytes=VMEM_A

time: 149 us -> 146 us (0.980)
  Pallas kernels: 147 us -> 145 us
    pallas_call x1, Pallas kernels: 81.9 us -> 78.2 us  [run_a(): pl.pallas_call(kernel_a, name='state_and_gradient', out_shape=(jax.ShapeD...]
where the time goes in v6:
time: 146 us
  Pallas kernels  145 us (99%)
    pallas_call x1, Pallas kernels, run_a(): pl.pallas_call(kernel_a, name='state_and_gradient', out_shape=(jax.ShapeD...  78.2 us
    pallas_call x1, Pallas kernels, run_c(): pl.pallas_call(kernel_c, name='weights_and_product', out_shape=jax.ShapeD...  57.4 us
    pallas_call x1, Pallas kernels, run_b(): pl.pallas_call(kernel_b, name='place_and_adam', out_shape=(state, state,...  9.27 us

profile of v6, /device:TPU:8, one launch (start us, length us, event | category | flops | bytes accessed | tf_op | source)
XLA Modules:
  0.0 146.4 jit_solution(9062887388283183537)
XLA Ops:
  0.6 78.2 %state_and_gradient.1 = (bf16[16,144,384]{2,1,0:T(8,128)(2,1)}, bf16[4,2,48,384]{3,2,1,0:T(8,128)(2,1)}, bf16[4,768,1024]{2,1,0:T(8,128)(2,1)}) custom-call(f32[192,4,384]{2,1,0:T(4,128)} %bitcast.12, f32[192,4,384]{2,1,0:T(4,128)} %bitcast.13, f32[192,4,384]{2,1,0:T(4,128)} %bitcast.14, bf16[256,768]{1,0:T(8,128)(2,1)} %ctx.1, bf16[256,6144]{1,0:T(8,128)(2,1)} %og.1, ...), custom_call_target="tpu_custom_call" | custom-call | flops 2415919104 | bytes 16777216 | tf_op jit(solution)/shard_map/state_and_gradient/pallas_call | solution.py:321
  78.9 9.3 %place_and_adam.1 = (f32[24,6144]{1,0:T(8,128)}, f32[24,6144]{1,0:T(8,128)}, f32[24,6144]{1,0:T(8,128)}, bf16[32,8,48,128]{3,2,1,0:T(8,128)(2,1)}) custom-call(s32[128]{0:T(128)} %bitcast.15, s32[128]{0:T(128)} %bitcast.16, bf16[2304,384]{1,0:T(8,128)(2,1)} %bitcast.17, bf16[4,2,48,384]{3,2,1,0:T(8,128)(2,1)} %get-tuple-element.12.gq_in), custom_call_target="tpu_custom_call" | custom-call | flops 1000000000 | bytes 5242880 | tf_op jit(solution)/shard_map/place_and_adam/pallas_call | solution.py:474
  88.1 57.4 %weights_and_product.1 = bf16[512,768]{1,0:T(8,128)(2,1)S(1)} custom-call(bf16[32,8,48,128]{3,2,1,0:T(8,128)(2,1)} %get-tuple-element.16.wb, bf16[4,768,1024]{2,1,0:T(8,128)(2,1)} %get-tuple-element.17.nc), custom_call_target="tpu_custom_call" | custom-call | flops 4831838208 | bytes 8388608 | tf_op jit(solution)/shard_map/weights_and_product/pallas_call | solution.py:643
  145.5 0.9 copy.13

commit v7 on v6

--- a/solution.py
+++ b/solution.py
@@ -33,8 +33,8 @@
     )
 
 
-SUBS = (4, 2, 2)
-STAGGER = 2
+SUBS = (4, 4, 4)
+STARTS = (0, 2, 4)
 ROOM = 32
 PARTS = 3
 VMEM_A = 60 * 2**20
@@ -261,8 +261,6 @@
             pass_state(pair)
         for k in ((), (1,), (3,))[s - 1]:
             tokens_passed(k)
-
-    tokens_passed(2)
 
     def out_copy(k, h):
         to = lax.rem(y + k, NY)
@@ -285,6 +283,7 @@
                 own_out.append(pltpu.make_async_copy(ysb.at[0, h], gq.at[y, h], loc_sem.at[3 + h]))
                 own_out[-1].start()
 
+    tokens_passed(2)
     for k in (1, 2, 3):
         og_copy(k).wait_send()
         ctx_copy(k).wait_send()
@@ -411,21 +410,21 @@
         rank = lo[i]
         start = starts[rank]
         length = pc[rank]
-        tile = start // 128
-        offset = lax.rem(start, 128)
+        tile = start >> 7
+        offset = start & 127
         keep = (lane >= offset) & (lane < offset + length)
         spill = lane < offset + length - 128
-        k = lax.rem(z + NZ - lax.rem(i // 4, NZ), NZ)
-        far = k // 4
-        pair = lax.rem(NY + (2 * far - 1) * k, NY)
-        slot = (i // 32) * NZ + 2 * pair + far
-        base = slot * SROWS + lax.rem(i, 4)
+        k = (z - (i >> 2)) & 7
+        far = k >> 2
+        pair = ((2 * far - 1) * k) & 3
+        slot = (i >> 5) * NZ + 2 * pair + far
+        base = slot * SROWS + (i & 3)
         for a in range(3):
             low, middle, high = (zbuf[tile, pl.ds(base + a * BAND, 8, stride=4), :] for tile in range(3))
             for r, value in enumerate(
                 (low, jnp.where(lane >= 96, low, middle), jnp.where(lane >= 64, middle, high), high)
             ):
-                value = pltpu.roll(value, lax.rem(offset + 32 * r, 128), 1)
+                value = pltpu.roll(value, (offset + 32 * r) & 127, 1)
                 pltpu.store(obuf.at[a * 4 + r, tile], value, mask=keep)
                 pltpu.store(obuf.at[a * 4 + r, tile + 1], value, mask=spill)
 
@@ -594,9 +593,9 @@
             po[n, 4 + d] = (held[n, d] + ro[n, d].astype(F32)).astype(BF)
             back(4 + d, n).start()
 
-    for tick in range(6 + STAGGER * (PARTS - 1)):
+    for tick in range(6 + STARTS[-1]):
         for n in range(PARTS):
-            s = tick - STAGGER * n
+            s = tick - STARTS[n]
             if s == 0:
                 for k in range(1, NT):
                     first_copy(k, n).wait_recv()
@@ -607,12 +606,12 @@
                     if 0 <= s < steps(d, part):
                         around(d, s, n, part).start()
         for n in range(PARTS):
-            if tick - STAGGER * n == 4:
+            if tick - STARTS[n] == 4:
                 if n == 0:
                     load.wait()
                 arrange(n)
                 multiply(n)
-            if tick - STAGGER * n == 5:
+            if tick - STARTS[n] == 5:
                 join(n)
 
     for n in range(PARTS):

time: 146 us -> 144 us (0.986)
  Pallas kernels: 145 us -> 142 us
    pallas_call x1, Pallas kernels: 9.27 us -> 6.54 us  [run_b(): pl.pallas_call(kernel_b, name='place_and_adam', out_shape=(state, state,...]
where the time goes in v7:
time: 144 us; the launch traced here: 143 us
  Pallas kernels  142 us (99%)
    pallas_call x1, Pallas kernels, run_a(): pl.pallas_call(kernel_a, name='state_and_gradient', out_shape=(jax.ShapeD...  78.2 us
    pallas_call x1, Pallas kernels, run_c(): pl.pallas_call(kernel_c, name='weights_and_product', out_shape=jax.ShapeD...  57 us
    pallas_call x1, Pallas kernels, run_b(): pl.pallas_call(kernel_b, name='place_and_adam', out_shape=(state, state,...  6.54 us

profile of v7, /device:TPU:8, one launch (start us, length us, event | category | flops | bytes accessed | tf_op | source)
XLA Modules:
  0.0 143.3 jit_solution(14792775057838358644)
XLA Ops:
  0.6 78.2 %state_and_gradient.1 = (bf16[16,144,384]{2,1,0:T(8,128)(2,1)}, bf16[4,2,48,384]{3,2,1,0:T(8,128)(2,1)}, bf16[4,768,1024]{2,1,0:T(8,128)(2,1)}) custom-call(f32[192,4,384]{2,1,0:T(4,128)} %bitcast.12, f32[192,4,384]{2,1,0:T(4,128)} %bitcast.13, f32[192,4,384]{2,1,0:T(4,128)} %bitcast.14, bf16[256,768]{1,0:T(8,128)(2,1)} %ctx.1, bf16[256,6144]{1,0:T(8,128)(2,1)} %og.1, ...), custom_call_target="tpu_custom_call" | custom-call | flops 2415919104 | bytes 16777216 | tf_op jit(solution)/shard_map/state_and_gradient/pallas_call | solution.py:320
  78.9 6.5 %place_and_adam.1 = (f32[24,6144]{1,0:T(8,128)}, f32[24,6144]{1,0:T(8,128)}, f32[24,6144]{1,0:T(8,128)}, bf16[32,8,48,128]{3,2,1,0:T(8,128)(2,1)}) custom-call(s32[128]{0:T(128)} %bitcast.15, s32[128]{0:T(128)} %bitcast.16, bf16[2304,384]{1,0:T(8,128)(2,1)} %bitcast.17, bf16[4,2,48,384]{3,2,1,0:T(8,128)(2,1)} %get-tuple-element.12.gq_in), custom_call_target="tpu_custom_call" | custom-call | flops 1000000000 | bytes 5242880 | tf_op jit(solution)/shard_map/place_and_adam/pallas_call | solution.py:473
  85.4 57.0 %weights_and_product.1 = bf16[512,768]{1,0:T(8,128)(2,1)S(1)} custom-call(bf16[32,8,48,128]{3,2,1,0:T(8,128)(2,1)} %get-tuple-element.16.wb, bf16[4,768,1024]{2,1,0:T(8,128)(2,1)} %get-tuple-element.17.nc), custom_call_target="tpu_custom_call" | custom-call | flops 4831838208 | bytes 8388608 | tf_op jit(solution)/shard_map/weights_and_product/pallas_call | solution.py:642
  142.4 0.9 copy.13
